TPU v7x, 512 devices: a whole 4x4x16 slice. The times are simulated.
512 devices in a mesh: chan: 4 (over y_hi, core), row: 128 (over x, y_lo, z).
Axes of the slice: x: 4, y: 4 (y_hi: 2, y_lo: 2; y = y_hi * 2 + y_lo), z: 16, core: 2. Of those that a mesh axis runs over, the one named last changes fastest.
Arguments:
- amplitudes: bfloat16 [4, 2048, 256], P('chan', 'row'), may hold values from -6 to 6
- ladder_pp: bfloat16 [4, 2048, 2048], P('chan', 'row'), may hold values from -0.125 to 0.125
- cycle_proton: bfloat16 [4, 2048, 2048], P('chan', 'row'), may hold values from -0.125 to 0.125
- cycle_neutron: bfloat16 [4, 256, 256], P('chan', 'row'), may hold values from -0.375 to 0.375
- recouple: float32 [4, 4], replicated, may hold values from -3 to 3
- proton_live: int32 [4], replicated, may hold values from 2 to 128, as said below
Outputs:
- residual: bfloat16 [4, 2048, 256], P('chan', 'row')
Inputs may be any that keep to these rules, and one draw needn't show every extreme that they name: `proton_live`: live proton particle orbitals of each channel; some channel uses all 128.
All inputs are finite; a program needn't handle non-finite values.
Results may differ from a plain program's by a relative error of at most 0.00125.
Values may be sent and summed in bfloat16 or wider, within the bound.
A program may use at most 128 MiB of HBM per device.

v0:
```python
import jax
import jax.numpy as jnp
from jax import lax
from jax.sharding import PartitionSpec as P

NB = 16
NI = 16
NJ = 16


def proton_input(shard_piece):
    per_dev = shard_piece.shape[0]
    orbit_count = shard_piece.shape[1]
    shaped = shard_piece.reshape(per_dev, orbit_count, NB, NI, NJ)
    return shaped.transpose(0, 1, 3, 2, 4).reshape(per_dev, orbit_count * NI, NB * NJ)


def neutron_input(shard_piece):
    per_dev = shard_piece.shape[0]
    orbit_count = shard_piece.shape[1]
    shaped = shard_piece.reshape(per_dev, orbit_count, NB, NI, NJ)
    return shaped.transpose(0, 2, 4, 1, 3).reshape(per_dev, NB * NJ, orbit_count * NI)


def ladder_piece(ladder_pp, shard_piece):
    per_dev = shard_piece.shape[0]
    orbit_count = shard_piece.shape[1]
    flat_piece = shard_piece.reshape(per_dev, orbit_count * NB, NI * NJ)
    return jnp.einsum("cpq,cqh->cph", ladder_pp, flat_piece, preferred_element_type=jnp.float32)


def local(amplitudes, ladder_pp, cycle_proton, cycle_neutron, recouple, proton_live):
    per_dev = amplitudes.shape[0]
    local_rows = amplitudes.shape[1]
    proton_block = local_rows // NB
    chan_index = lax.axis_index("chan")
    row_index = lax.axis_index("row")
    live_here = lax.dynamic_slice_in_dim(proton_live, chan_index * per_dev, per_dev)
    proton_index = row_index * proton_block + jnp.arange(local_rows, dtype=jnp.int32) // NB
    live_mask = proton_index[None, :] < live_here[:, None]
    masked = jnp.where(live_mask[:, :, None], amplitudes, jnp.zeros_like(amplitudes))
    packed = masked.reshape(per_dev, proton_block, NB * NI * NJ)
    channel_all = lax.all_gather(packed, "chan", axis=0, tiled=True)
    mixing = lax.dynamic_slice_in_dim(recouple, chan_index * per_dev, per_dev, 0)
    blended = jnp.einsum(
        "cd,dar->car", mixing, channel_all.astype(jnp.float32), precision=lax.Precision.HIGHEST
    )
    plain_rows = lax.all_gather(packed.astype(jnp.float32), "row", axis=1, tiled=True).astype(
        jnp.bfloat16
    )
    blend_rows = lax.all_gather(blended, "row", axis=1, tiled=True)
    ladder_sum = ladder_piece(ladder_pp, plain_rows)
    proton_sum = jnp.einsum(
        "cxy,cyz->cxz",
        cycle_proton,
        proton_input(blend_rows),
        precision=lax.Precision.HIGHEST,
        preferred_element_type=jnp.float32,
    )
    neutron_block = jnp.einsum(
        "cxy,cyz->cxz",
        cycle_neutron,
        neutron_input(blend_rows),
        precision=lax.Precision.HIGHEST,
        preferred_element_type=jnp.float32,
    )
    neutron_sum = neutron_block
    ladder_sum, proton_sum, neutron_sum = (ladder_sum, proton_sum, neutron_sum)
    proton_back = (
        proton_sum.reshape(per_dev, proton_block, NI, NB, NJ)
        .transpose(0, 1, 3, 2, 4)
        .reshape(per_dev, local_rows, NI * NJ)
    )
    neutron_moved = lax.all_to_all(neutron_sum, "row", split_axis=2, concat_axis=1, tiled=True)
    neutron_back = (
        neutron_moved.reshape(per_dev, NB, NJ, proton_block, NI)
        .transpose(0, 3, 1, 4, 2)
        .reshape(per_dev, local_rows, NI * NJ)
    )
    combined = ladder_sum + proton_back + neutron_back
    return jnp.where(live_mask[:, :, None], combined, jnp.float32(0.0)).astype(jnp.bfloat16)


def solution(mesh):
    in_specs = (
        P("chan", "row", None),
        P("chan", "row", None),
        P("chan", "row", None),
        P("chan", "row", None),
        P(),
        P(),
    )
    out_specs = P("chan", "row", None)
    return jax.shard_map(local, mesh=mesh, in_specs=in_specs, out_specs=out_specs, check_vma=False)
```

profile of v0, /device:TPU:64, one launch (start us, length us, event | category | flops | bytes accessed | tf_op | source)
XLA Modules:
  0.0 1314.2 jit_solution(17762970895003572832)
XLA Ops:
  6.5 0.0 copy-start
  6.5 0.0 all-gather.4.cloned.1.call-start
  6.5 1.3 dynamic_slice.6
  7.8 0.7 fusion.10
  8.5 0.8 broadcast_select_fusion
  9.2 0.6 reshape.99
  9.9 0.0 all-gather.4.cloned.1.call-update
  9.9 0.0 all-gather.6.cloned.1.call-start
  9.9 7.0 all_gather.10
  16.9 1.5 fusion.7
  18.4 0.0 all-gather.6.cloned.1.call-update
  18.4 581.9 %all-gather.4.cloned.1.call-done = bf16[1,128,4096]{2,0,1:T(2,128)(2,1)} async-done(((bf16[1,1,4096]{2,0,1:T(2,128)(2,1)}), bf16[1,128,4096]{2,0,1:T(2,128)(2,1)}) %all-gather.4.cloned.1.call-update) | async-done | bytes 1048592 | tf_op jit(solution)/shard_map/all_gather | solution.py:48
  600.3 7.8 convert_reduce_fusion
  608.2 0.7 reshape.100
  608.9 573.9 %all-gather.6.cloned.1.call-done = f32[524288]{0:T(1024)} async-done(((f32[4096]{0:T(1024)}), f32[524288]{0:T(1024)}) %all-gather.6.cloned.1.call-update) | async-done | bytes 2097168 | tf_op jit(solution)/shard_map/all_gather | solution.py:51
  1182.8 10.5 reshape.104
  1193.3 15.7 %copy.25 = f32[1,128,16,16,16]{4,3,2,1,0:T(8,128)} copy(f32[1,128,16,16,16]{4,2,3,1,0:T(8,128)} %bitcast.64) | data formatting | bytes 4194304 | tf_op jit(solution)/shard_map/transpose | solution.py:15
  1209.0 11.4 reshape.105
  1220.4 1.9 copy.26
  1222.2 19.8 %copy.28 = f32[1,16,16,128,16]{4,3,2,1,0:T(8,128)} copy(f32[1,16,16,128,16]{2,4,1,3,0:T(8,128)} %bitcast.65) | data formatting | bytes 4194304 | tf_op jit(solution)/shard_map/transpose | solution.py:22
  1242.0 0.0 copy-start.3
  1242.0 14.2 %reshape.108 = f32[256,2048]{1,0:T(8,128)S(1)} reshape(f32[1,16,16,128,16]{4,3,2,1,0:T(8,128)} %copy.28) | data formatting | bytes 4194304 | tf_op jit(solution)/shard_map/reshape.24
  1256.2 0.0 copy-done.3
  1256.2 0.8 convolution_bitcast_fusion
  1257.0 0.0 copy-start.1
  1257.0 1.9 copy.29
  1258.9 10.4 all-to-all-start
  1269.3 0.0 copy-done
  1269.3 0.0 copy-done.1
  1269.3 0.0 copy-start.2
  1269.3 1.1 convolution_bitcast_fusion.1
  1270.4 0.1 copy.27
  1270.5 0.1 reshape.107
  1270.6 33.4 %all-to-all-done = f32[1,2,2048]{1,0,2:T(1,128)} async-done(((f32[1,2,2048]{1,0,2:T(1,128)}), f32[1,2,2048]{1,0,2:T(1,128)}, u32[]{:S(2)}, u32[]{:S(2)}) %all-to-all-start) | async-done | bytes 16416 | tf_op jit(solution)/shard_map/all_to_all | solution.py:74
  1304.1 2.1 copy.33
  1306.2 0.1 copy.31
  1306.3 0.1 copy.32
  1306.4 0.1 reshape.111
  1306.5 0.0 copy-done.2
  1306.5 0.9 fusion.4
Async XLA Ops:
  6.5 1262.8 %copy-start = (bf16[1,16,2048]{2,1,0:T(8,128)(2,1)S(1)}, bf16[1,16,2048]{2,1,0:T(8,128)(2,1)}, u32[]{:S(2)}) copy-start(bf16[1,16,2048]{2,1,0:T(8,128)(2,1)} %param.8) | copy-start | bytes 196612
  6.5 593.8 %all-gather.4.cloned.1.call-start = ((), (), s32[]{:S(2)}) async-start(), calls=%async_computation.1 | async-start | bytes 2113536 | tf_op jit(solution)/shard_map/all_gather | solution.py:48
  9.9 1172.9 %all-gather.6.cloned.1.call-start = ((), (), s32[]{:S(2)}) async-start(), calls=%async_computation.2 | async-start | bytes 2113536 | tf_op jit(solution)/shard_map/all_gather | solution.py:51
  1242.0 14.2 %copy-start.3 = (bf16[1,2,256]{2,1,0:T(2,128)(2,1)S(1)}, bf16[1,2,256]{2,1,0:T(2,128)(2,1)}, u32[]{:S(2)}) copy-start(bf16[1,2,256]{2,1,0:T(2,128)(2,1)} %param.9) | copy-start | bytes 3076
  1257.0 12.3 copy-start.1
  1258.9 45.2 %all-to-all-start = ((f32[1,2,2048]{1,0,2:T(1,128)}), f32[1,2,2048]{1,0,2:T(1,128)}, u32[]{:S(2)}, u32[]{:S(2)}) async-start(f32[1,2,2048]{1,0,2:T(1,128)} %copy.29), calls=%async_computation | async-start | bytes 2097152 | tf_op jit(solution)/shard_map/all_to_all | solution.py:74
  1269.3 37.2 %copy-start.2 = (bf16[1,16,2048]{2,1,0:T(8,128)(2,1)S(1)}, bf16[1,16,2048]{2,1,0:T(8,128)(2,1)}, u32[]{:S(2)}) copy-start(bf16[1,16,2048]{2,1,0:T(8,128)(2,1)} %param.7) | copy-start | bytes 196612
Sparse Core Ops, SparseCore 0:
  10.0 590.2 all-gather.3
  602.4 580.3 all-gather.5
where the time goes:
time: 1320 us; the launch traced here: 1310 us
  waiting for transfers between devices  1190 us (90%)
  local copies, waits for them, and re-layouts  88.4 us (7%)
  between operations  13.5 us (1%)
    all_gather x1, waiting for transfers between devices, local(): lax.all_gather(packed.astype(jnp.float32), 'row', axis=1, tiled=True)  582 us
    all_gather x1, waiting for transfers between devices, local(): blend_rows = lax.all_gather(blended, 'row', axis=1, tiled=True)  574 us
    all_to_all x1, waiting for transfers between devices, local(): lax.all_to_all(neutron_sum, 'row', split_axis=2, concat_axis=1, tiled=True)  33.4 us
  transfers between devices with their start and end apart: 3, of which 3 were waited for; matrix products, arithmetic and copies ran while one was open for 1% of the time, Pallas kernels for 0%

commit v1 on v0

v1 whole, which is shorter than its diff:
```python
import jax
import jax.numpy as jnp
from jax import lax
from jax.experimental import pallas as pl
from jax.experimental.pallas import tpu as pltpu
from jax.sharding import PartitionSpec as P

MESH = pl.DeviceIdType.MESH
F32 = jnp.float32
BF16 = jnp.bfloat16


def swap_rows_lanes(v):
    n, width = v.shape
    lane = lax.broadcasted_iota(jnp.int32, (1, 1, width), 2)
    row = lax.broadcasted_iota(jnp.int32, (1, 8, 1), 1)
    v = v.reshape(n // 8, 8, width)
    for s in range(3):
        step, reach = 1 << s, 8 << s
        lane_bit = (lane & reach) != 0
        row_bit = (row & step) != 0
        down = pltpu.roll(pltpu.roll(v, width - reach, 2), step, 1)
        up = pltpu.roll(pltpu.roll(v, reach, 2), 8 - step, 1)
        moved = jnp.where(row_bit, down, up)
        v = jnp.where(jnp.logical_xor(lane_bit, row_bit), moved, v)
    lane_bit = (lane & 64) != 0
    v = v.reshape(n // 16, 2, 8, width)
    low, high = v[:, 0], v[:, 1]
    new_low = jnp.where(lane_bit, pltpu.roll(high, 64, 2), low)
    new_high = jnp.where(lane_bit, high, pltpu.roll(low, width - 64, 2))
    return jnp.stack([new_low, new_high], axis=1).reshape(n, width)


def lanes_by_half():
    old = lax.broadcasted_iota(jnp.int32, (256, 256), 0)
    new = lax.broadcasted_iota(jnp.int32, (256, 256), 1)
    goes = ((old >> 3) & 1) * 128 + (old >> 4) * 8 + (old & 7)
    return jnp.where(goes == new, 1.0, 0.0).astype(BF16)


def lanes_back():
    new = lax.broadcasted_iota(jnp.int32, (256, 256), 0)
    old = lax.broadcasted_iota(jnp.int32, (256, 256), 1)
    goes = ((old >> 3) & 1) * 128 + (old >> 4) * 8 + (old & 7)
    return jnp.where(goes == new, 1.0, 0.0).astype(BF16)


def neutron_row_order():
    new = lax.broadcasted_iota(jnp.int32, (256, 256), 0)
    old = lax.broadcasted_iota(jnp.int32, (256, 256), 1)
    z, t = old >> 4, old & 1
    b = ((old >> 1) & 7) * 2 + (z >> 3)
    goes = ((z >> 2) & 1) * 128 + b * 8 + (z & 3) * 2 + t
    return jnp.where(goes == new, 1.0, 0.0).astype(BF16)


def mm(a, b):
    return jnp.dot(a, b, preferred_element_type=F32)


def kernel(
    amp, lad, cyc, neu, rec, live, out,
    amp_v, neu_v, zbuf, sall, n1, nall, wl, wc, abuf, fsend, frecv,
    in_sem, own_sem, z_s, z_r, s_s, s_r, n1_s, n1_r, n2_s, n2_r,
    wl_s, wl_r, wc_s, wc_r, a_s, a_r, f_s, f_r,
):
    e, r = lax.axis_index("chan"), lax.axis_index("row")
    yh, co = lax.div(e, 2), lax.rem(e, 2)
    x, yl, z = lax.div(r, 32), lax.rem(lax.div(r, 16), 2), lax.rem(r, 16)
    me = e * 4 + x

    def at_z(k):
        return (e, x * 32 + yl * 16 + lax.rem(z + k + 16, 16))

    def member(k):
        m = lax.rem(me + k, 16)
        return lax.div(m, 4), lax.rem(m, 4)

    def near_z(k):
        return (4 - lax.div(k, 2)) * (1 - 2 * lax.rem(k, 2))

    bar = pltpu.get_barrier_semaphore()

    def greet(dev):
        pl.semaphore_signal(bar, inc=1, device_id=dev, device_id_type=MESH)

    @pl.loop(0, 8)
    def _(k):
        greet(at_z(near_z(k)))

    @pl.loop(1, 16)
    def _(k):
        pe, px = member(k)
        greet((pe, px * 32 + yl * 16 + z))

    @pl.loop(0, 4)
    def _(k):
        greet((k, x * 32 + (1 - yl) * 16 + z))

    @pl.loop(1, 4)
    def _(k):
        greet((e, lax.rem(x + k, 4) * 32 + (1 - yl) * 16 + z))

    get_amp = pltpu.make_async_copy(amp.at[0], amp_v, in_sem.at[0])
    get_neu = pltpu.make_async_copy(neu, neu_v, in_sem.at[1])
    get_amp.start()
    get_neu.start()
    my_rows = pl.ds(pl.multiple_of(me * 16, 16), 16)
    my_cols = pl.ds(pl.multiple_of(x * 512 + yh * 256, 256), 256)
    own_l = pltpu.make_async_copy(lad.at[0, :, my_cols], wl.at[my_rows], own_sem.at[0])
    own_c = pltpu.make_async_copy(cyc.at[0, :, my_cols], wc.at[my_rows], own_sem.at[1])
    own_l.start()
    own_c.start()

    order = lanes_by_half()
    alive = jnp.where(r < live[e], 1.0, 0.0).astype(F32)
    my_z = pl.ds(pl.multiple_of(z * 16, 16), 16)
    my_e = pl.ds(pl.multiple_of(e * 16, 16), 16)
    group = x * 2 + yl
    get_amp.wait()
    block = mm((amp_v[...].astype(F32) * alive).astype(BF16), order)
    zbuf[my_z, :] = block.astype(BF16)
    sall[my_e, :] = swap_rows_lanes(block).astype(BF16)
    get_neu.wait()
    pair = mm(neu_v[0], order)
    place = lax.broadcasted_iota(jnp.int32, (16, 256), 0)
    padded = jnp.where(
        place == 2 * group, pair[0:1], jnp.where(place == 2 * group + 1, pair[1:2], 0.0)
    )
    n1[group] = padded.astype(BF16)

    pl.semaphore_wait(bar, 30)

    def send(src, dst, ss, rs, dev):
        return pltpu.make_async_remote_copy(
            src_ref=src, dst_ref=dst, send_sem=ss, recv_sem=rs,
            device_id=dev, device_id_type=MESH,
        )

    def z_rows(k):
        return pl.ds(pl.multiple_of(lax.rem(z + k + 16, 16) * 16, 16), 16)

    def z_copy(buf, ss, rs, slot, source, to):
        rows = z_rows(source)
        return send(
            buf.at[rows], buf.at[rows], ss.at[slot],
            rs.at[lax.rem(z + source + 16, 16)], at_z(to),
        )

    def z_start(buf, ss, rs):
        @pl.loop(0, 8)
        def _(k):
            z_copy(buf, ss, rs, k, 0, near_z(k)).start()

    def z_wait(buf, ss, rs, source):
        z_copy(buf, ss, rs, 0, source, 1).wait_recv()

    def z_relay(buf, ss, rs):
        z_wait(buf, ss, rs, -4)

        @pl.loop(0, 4)
        def _(k):
            z_copy(buf, ss, rs, 8 + k, -4, 4 - k).start()

        z_wait(buf, ss, rs, 4)

        @pl.loop(0, 3)
        def _(k):
            z_copy(buf, ss, rs, 12 + k, 4, k - 3).start()

    def z_sent(buf, ss, rs):
        @pl.loop(0, 15)
        def _(k):
            z_copy(buf, ss, rs, k, 0, 1).wait_send()

    def n1_copy(k):
        g = lax.rem(group + k, 8)
        dev = (e, lax.div(g, 2) * 32 + lax.rem(g, 2) * 16 + z)
        return send(n1.at[group], n1.at[group], n1_s.at[k], n1_r.at[group], dev)

    def s_copy(k):
        rows = sall.at[my_e]
        return send(rows, rows, s_s.at[k], s_r.at[e], (lax.rem(e + k, 4), r))

    def w_copy(src, dst, ss, rs, k):
        pe, px = member(k)
        cols = pl.ds(pl.multiple_of(px * 512 + lax.div(pe, 2) * 256, 256), 256)
        return send(
            src.at[0, :, cols], dst.at[my_rows], ss.at[k], rs.at[me],
            (pe, px * 32 + yl * 16 + z),
        )

    z_start(zbuf, z_s, z_r)

    @pl.loop(1, 8)
    def _(k):
        n1_copy(k).start()

    @pl.loop(1, 4)
    def _(k):
        s_copy(k).start()

    @pl.loop(1, 16)
    def _(k):
        w_copy(lad, wl, wl_s, wl_r, k).start()
        w_copy(cyc, wc, wc_s, wc_r, k).start()

    z_relay(zbuf, z_s, z_r)

    @pl.loop(1, 8)
    def _(k):
        g = lax.rem(group + k, 8)
        send(n1.at[g], n1.at[g], n1_s.at[k], n1_r.at[g], at_z(1)).wait_recv()

    gathered = n1[0].astype(F32)
    for g in range(1, 8):
        gathered = gathered + n1[g].astype(F32)
    nall[my_z, :] = gathered.astype(BF16)
    z_start(nall, n2_s, n2_r)

    def quarter(t):
        return lax.rem(lax.div(z, 4) + t + 4, 4)

    def a_copy(q, k, t):
        pco, pyl = lax.rem(k, 2), lax.div(k, 2)
        rows = pl.ds(pl.multiple_of(q * 64, 64), 64)
        src = zbuf.at[rows, pl.ds(pl.multiple_of(pco * 128, 128), 128)]
        dst = abuf.at[e, rows]
        return src, dst, a_s.at[t, k], a_r.at[e, q], (yl * 2 + pco, x * 32 + pyl * 16 + z)

    def is_self(k):
        pco, pyl = lax.rem(k, 2), lax.div(k, 2)
        return jnp.logical_and(yh == yl, jnp.logical_and(pco == co, pyl == yl))

    def a_start(t, turn):
        q = quarter(turn)

        @pl.loop(0, 4)
        def _(i):
            away = lax.rem(q * 4 + i - z + 16, 16)
            fresh = jnp.logical_and(away != 0, jnp.logical_and(away != 4, away != 12))

            @pl.when(fresh)
            def _():
                z_wait(zbuf, z_s, z_r, away)

        @pl.loop(0, 4)
        def _(k):
            src, dst, ss, rs, dev = a_copy(q, k, t)
            own = is_self(k)

            @pl.when(own)
            def _():
                pltpu.make_async_copy(src, dst, rs).start()

            @pl.when(jnp.logical_not(own))
            def _():
                send(src, dst, ss, rs, dev).start()

    def a_sent(t):
        @pl.loop(0, 4)
        def _(k):
            src, dst, ss, rs, dev = a_copy(0, k, t)

            @pl.when(jnp.logical_not(is_self(k)))
            def _():
                send(src, dst, ss, rs, dev).wait_send()

    def a_wait(turn):
        q = quarter(turn)
        rows = pl.ds(pl.multiple_of(q * 64, 64), 64)

        @pl.loop(0, 4)
        def _(c):
            dst = abuf.at[c, rows]
            send(dst, dst, a_s.at[0, 0], a_r.at[c, q], at_z(1)).wait_recv()

    a_start(0, 0)
    a_start(1, 1)
    a_start(2, 3)
    z_relay(nall, n2_s, n2_r)
    a_start(3, 2)

    own_l.wait()
    own_c.wait()

    @pl.loop(1, 16)
    def _(k):
        m = lax.rem(me + k, 16)
        rows = pl.ds(pl.multiple_of(m * 16, 16), 16)
        send(wl.at[rows], wl.at[rows], wl_s.at[k], wl_r.at[m], at_z(1)).wait_recv()
        send(wc.at[rows], wc.at[rows], wc_s.at[k], wc_r.at[m], at_z(1)).wait_recv()

    for turn in (0, 1, 3, 2):
        a_wait(turn)

    products = []
    for c in range(4):
        turned = swap_rows_lanes(abuf[c].astype(F32)).astype(BF16)
        products.append(mm(wc[...], turned))
    for c in range(4):
        rows = slice(64 * c, 64 * c + 64)
        mixed = rec[c, 0] * products[0][rows]
        for d in range(1, 4):
            mixed = mixed + rec[c, d] * products[d][rows]
        fsend[rows, :] = swap_rows_lanes(mixed) + mm(wl[rows, :], abuf[c])

    def f_copy(k):
        m = lax.rem(me + k, 16)
        rows = pl.ds(pl.multiple_of(m * 16, 16), 16)
        return send(
            fsend.at[rows], frecv.at[me], f_s.at[k], f_r.at[me],
            (lax.div(m, 4), lax.rem(m, 4) * 32 + yl * 16 + z),
        )

    @pl.loop(1, 16)
    def _(k):
        f_copy(k).start()

    frecv[me] = fsend[my_rows, :]

    @pl.loop(1, 4)
    def _(k):
        c = lax.rem(e + k, 4)
        rows = sall.at[pl.ds(pl.multiple_of(c * 16, 16), 16)]
        send(rows, rows, s_s.at[k], s_r.at[c], at_z(1)).wait_recv()

    @pl.loop(1, 16)
    def _(k):
        @pl.when(jnp.logical_and(k != 4, k != 12))
        def _():
            z_wait(nall, n2_s, n2_r, k)

    sorted_rows = mm(neutron_row_order(), nall[...]).astype(BF16)
    terms = lax.dot_general(
        sall[...], sorted_rows, (((1,), (1,)), ((), ())), preferred_element_type=F32
    )
    neutron = rec[e, 0] * terms[0:16]
    for c in range(1, 4):
        neutron = neutron + rec[e, c] * terms[16 * c : 16 * c + 16]
    neutron = swap_rows_lanes(neutron)
    back = lanes_back()

    @pl.loop(1, 16)
    def _(k):
        m = lax.rem(me + k, 16)
        dst = frecv.at[m]
        send(fsend.at[pl.ds(0, 16)], dst, f_s.at[k], f_r.at[m], at_z(1)).wait_recv()

    halves = []
    for h in range(2):
        total = neutron[:, 128 * h : 128 * h + 128]
        for s in range(2):
            for i in range(4):
                total = total + frecv[(2 * s + h) * 4 + i]
        halves.append((total * alive).astype(BF16))
    result = lax.dot_general(
        jnp.concatenate(halves, axis=1), back, (((1,), (0,)), ((), ())),
        preferred_element_type=F32,
    )
    out[0] = result.astype(BF16)

    z_sent(zbuf, z_s, z_r)
    z_sent(nall, n2_s, n2_r)
    for t in range(4):
        a_sent(t)

    @pl.loop(1, 8)
    def _(k):
        n1_copy(k).wait_send()

    @pl.loop(1, 4)
    def _(k):
        s_copy(k).wait_send()

    @pl.loop(1, 16)
    def _(k):
        w_copy(lad, wl, wl_s, wl_r, k).wait_send()
        w_copy(cyc, wc, wc_s, wc_r, k).wait_send()
        f_copy(k).wait_send()


def local(amplitudes, ladder_pp, cycle_proton, cycle_neutron, recouple, proton_live):
    dma = pltpu.SemaphoreType.DMA
    return pl.pallas_call(
        kernel,
        out_shape=jax.ShapeDtypeStruct((1, 16, 256), BF16),
        in_specs=[pl.BlockSpec(memory_space=pl.ANY)] * 4
        + [pl.BlockSpec(memory_space=pltpu.SMEM)] * 2,
        out_specs=pl.BlockSpec(memory_space=pltpu.VMEM),
        scratch_shapes=[
            pltpu.VMEM((16, 256), BF16),
            pltpu.VMEM((1, 2, 256), BF16),
            pltpu.VMEM((256, 256), BF16),
            pltpu.VMEM((64, 256), BF16),
            pltpu.VMEM((8, 16, 256), BF16),
            pltpu.VMEM((256, 256), BF16),
            pltpu.VMEM((256, 256), BF16),
            pltpu.VMEM((256, 256), BF16),
            pltpu.VMEM((4, 256, 128), BF16),
            pltpu.VMEM((256, 128), F32),
            pltpu.VMEM((16, 16, 128), F32),
            dma((2,)),
            dma((2,)),
            dma((15,)),
            dma((16,)),
            dma((4,)),
            dma((4,)),
            dma((8,)),
            dma((8,)),
            dma((15,)),
            dma((16,)),
            dma((16,)),
            dma((16,)),
            dma((16,)),
            dma((16,)),
            dma((4, 4)),
            dma((4, 4)),
            dma((16,)),
            dma((16,)),
        ],
        compiler_params=pltpu.CompilerParams(
            collective_id=0, has_side_effects=True, vmem_limit_bytes=32 << 20
        ),
        name="pair_residual",
    )(amplitudes, ladder_pp, cycle_proton, cycle_neutron, recouple, proton_live)


def solution(mesh):
    rows = P("chan", "row", None)
    return jax.shard_map(
        local,
        mesh=mesh,
        in_specs=(rows, rows, rows, rows, P(), P()),
        out_specs=rows,
        check_vma=False,
    )
```

time: 1320 us -> 44.4 us (0.03)
  the two profiles are of different devices: /device:TPU:64 before, /device:TPU:1 now
where the time goes in v1:
time: 44.4 us; the launch traced here: 44.1 us
  Pallas kernels  39.1 us (88%)
  local copies, waits for them, and re-layouts  4.99 us (11%)
    pallas_call x1, Pallas kernels, local(): pl.pallas_call(kernel, out_shape=jax.ShapeDtypeStruct((1, 16, 256), BF16)...  39.1 us
    unnamed x13, local copies, waits for them, and re-layouts  4.99 us

profile of v1, /device:TPU:1, one launch (start us, length us, event | category | flops | bytes accessed | tf_op | source)
XLA Modules:
  0.0 44.1 jit_solution(7749173577206366806)
XLA Ops:
  0.0 0.0 copy-start
  0.0 0.8 %copy-done = bf16[1,16,2048]{2,1,0:T(8,128)(2,1)S(1)} copy-done((bf16[1,16,2048]{2,1,0:T(8,128)(2,1)S(1)}, bf16[1,16,2048]{2,1,0:T(8,128)(2,1)}, u32[]{:S(2)}) %copy-start) | copy-done | bytes 65560
  0.8 0.0 copy-start.1
  0.8 0.8 %copy-done.1 = bf16[1,16,2048]{2,1,0:T(8,128)(2,1)S(1)} copy-done((bf16[1,16,2048]{2,1,0:T(8,128)(2,1)S(1)}, bf16[1,16,2048]{2,1,0:T(8,128)(2,1)}, u32[]{:S(2)}) %copy-start.1) | copy-done | bytes 65560
  1.7 0.0 copy-start.2
  1.7 0.7 %copy-done.2 = bf16[1,16,256]{2,1,0:T(8,128)(2,1)S(1)} copy-done((bf16[1,16,256]{2,1,0:T(8,128)(2,1)S(1)}, bf16[1,16,256]{2,1,0:T(8,128)(2,1)}, u32[]{:S(2)}) %copy-start.2) | copy-done | bytes 8216
  2.4 0.0 copy-start.3
  2.4 0.7 %copy-done.3 = f32[4,4]{1,0:T(4,128)S(1)} copy-done((f32[4,4]{1,0:T(4,128)S(1)}, f32[4,4]{1,0:T(4,128)}, u32[]{:S(2)}) %copy-start.3) | copy-done | bytes 88
  3.1 0.0 copy-start.4
  3.1 0.7 %copy-done.4 = bf16[1,2,256]{2,1,0:T(2,128)(2,1)S(1)} copy-done((bf16[1,2,256]{2,1,0:T(2,128)(2,1)S(1)}, bf16[1,2,256]{2,1,0:T(2,128)(2,1)}, u32[]{:S(2)}) %copy-start.4) | copy-done | bytes 1048
  3.7 0.0 copy-start.5
  3.7 0.7 %copy-done.5 = s32[4]{0:T(128)S(1)} copy-done((s32[4]{0:T(128)S(1)}, s32[4]{0:T(128)}, u32[]{:S(2)}) %copy-start.5) | copy-done | bytes 40
  4.4 39.1 %pair_residual.1 = bf16[1,16,256]{2,1,0:T(8,128)(2,1)S(1)} custom-call(bf16[1,16,256]{2,1,0:T(8,128)(2,1)S(1)} %copy-done.2, bf16[1,16,2048]{2,1,0:T(8,128)(2,1)S(1)} %copy-done, bf16[1,16,2048]{2,1,0:T(8,128)(2,1)S(1)} %copy-done.1, bf16[1,2,256]{2,1,0:T(2,128)(2,1)S(1)} %copy-done.4, f32[4,4]{1,0:T(4,128)S(1)} %copy-done.3, s32[4]{0:T(128)S(1)} %copy-done.5), custom_call_target="tpu_custom_call" | custom-call | tf_op jit(solution)/shard_map/pair_residual/pallas_call | solution.py:385
  43.5 0.6 %copy.8 = bf16[1,16,256]{2,1,0:T(8,128)(2,1)} copy(bf16[1,16,256]{2,1,0:T(8,128)(2,1)S(1)} %pair_residual.1) | data formatting | bytes 16384
Async XLA Ops:
  0.0 0.8 %copy-start = (bf16[1,16,2048]{2,1,0:T(8,128)(2,1)S(1)}, bf16[1,16,2048]{2,1,0:T(8,128)(2,1)}, u32[]{:S(2)}) copy-start(bf16[1,16,2048]{2,1,0:T(8,128)(2,1)} %lad.1) | copy-start | bytes 196612
  0.8 0.8 %copy-start.1 = (bf16[1,16,2048]{2,1,0:T(8,128)(2,1)S(1)}, bf16[1,16,2048]{2,1,0:T(8,128)(2,1)}, u32[]{:S(2)}) copy-start(bf16[1,16,2048]{2,1,0:T(8,128)(2,1)} %cyc.1) | copy-start | bytes 196612
  1.7 0.7 %copy-start.2 = (bf16[1,16,256]{2,1,0:T(8,128)(2,1)S(1)}, bf16[1,16,256]{2,1,0:T(8,128)(2,1)}, u32[]{:S(2)}) copy-start(bf16[1,16,256]{2,1,0:T(8,128)(2,1)} %amp.1) | copy-start | bytes 24580
  2.4 0.7 %copy-start.3 = (f32[4,4]{1,0:T(4,128)S(1)}, f32[4,4]{1,0:T(4,128)}, u32[]{:S(2)}) copy-start(f32[4,4]{1,0:T(4,128)} %rec.1) | copy-start | bytes 196
  3.1 0.7 %copy-start.4 = (bf16[1,2,256]{2,1,0:T(2,128)(2,1)S(1)}, bf16[1,2,256]{2,1,0:T(2,128)(2,1)}, u32[]{:S(2)}) copy-start(bf16[1,2,256]{2,1,0:T(2,128)(2,1)} %neu.1) | copy-start | bytes 3076
  3.7 0.7 %copy-start.5 = (s32[4]{0:T(128)S(1)}, s32[4]{0:T(128)}, u32[]{:S(2)}) copy-start(s32[4]{0:T(128)} %live.1) | copy-start | bytes 52

commit v2 on v1

v2 whole, which is shorter than its diff:
```python
import jax
import jax.numpy as jnp
from jax import lax
from jax.experimental import pallas as pl
from jax.experimental.pallas import tpu as pltpu
from jax.sharding import PartitionSpec as P

MESH = pl.DeviceIdType.MESH
F32 = jnp.float32
BF16 = jnp.bfloat16


def swap_rows_lanes(v):
    n, width = v.shape
    lane = lax.broadcasted_iota(jnp.int32, (1, 1, width), 2)
    row = lax.broadcasted_iota(jnp.int32, (1, 8, 1), 1)
    v = v.reshape(n // 8, 8, width)
    for s in range(3):
        step, reach = 1 << s, 8 << s
        lane_bit = (lane & reach) != 0
        row_bit = (row & step) != 0
        down = pltpu.roll(pltpu.roll(v, width - reach, 2), step, 1)
        up = pltpu.roll(pltpu.roll(v, reach, 2), 8 - step, 1)
        moved = jnp.where(row_bit, down, up)
        v = jnp.where(jnp.logical_xor(lane_bit, row_bit), moved, v)
    lane_bit = (lane & 64) != 0
    v = v.reshape(n // 16, 2, 8, width)
    low, high = v[:, 0], v[:, 1]
    new_low = jnp.where(lane_bit, pltpu.roll(high, 64, 2), low)
    new_high = jnp.where(lane_bit, high, pltpu.roll(low, width - 64, 2))
    return jnp.stack([new_low, new_high], axis=1).reshape(n, width)


def lanes_by_half():
    old = lax.broadcasted_iota(jnp.int32, (256, 256), 0)
    new = lax.broadcasted_iota(jnp.int32, (256, 256), 1)
    goes = ((old >> 3) & 1) * 128 + (old >> 4) * 8 + (old & 7)
    return jnp.where(goes == new, 1.0, 0.0).astype(BF16)


def lanes_back():
    new = lax.broadcasted_iota(jnp.int32, (256, 256), 0)
    old = lax.broadcasted_iota(jnp.int32, (256, 256), 1)
    goes = ((old >> 3) & 1) * 128 + (old >> 4) * 8 + (old & 7)
    return jnp.where(goes == new, 1.0, 0.0).astype(BF16)


def neutron_row_order():
    new = lax.broadcasted_iota(jnp.int32, (256, 256), 0)
    old = lax.broadcasted_iota(jnp.int32, (256, 256), 1)
    z, t = (old >> 1) & 15, old & 1
    b = (old >> 5) * 2 + (z >> 3)
    goes = ((z >> 2) & 1) * 128 + b * 8 + (z & 3) * 2 + t
    return jnp.where(goes == new, 1.0, 0.0).astype(BF16)


def mm(a, b):
    return jnp.dot(a, b, preferred_element_type=F32)


NEAR, SLOTS = 9, 16
HERE = 4


def kernel(
    amp, lad, cyc, neu, rec_in, live_in, out,
    rec, live, amp_v, zbuf, nz, sall, nall, wl, wc, abuf, plain, turned, fsend, frecv,
    in_sem, own_sem, z_s, z_r, n_s, n_r, s_s, s_r, n1_s, n1_r,
    wl_s, wl_r, wc_s, wc_r, a_s, a_r, f_s, f_r,
):
    e, r = lax.axis_index("chan"), lax.axis_index("row")
    yh, co = lax.div(e, 2), lax.rem(e, 2)
    x, yl, z = lax.div(r, 32), lax.rem(lax.div(r, 16), 2), lax.rem(r, 16)
    me = e * 4 + x
    group = x * 2 + yl

    get_amp = pltpu.make_async_copy(amp.at[0], amp_v, in_sem.at[0])
    get_live = pltpu.make_async_copy(live_in, live, in_sem.at[1])
    get_rec = pltpu.make_async_copy(rec_in, rec, in_sem.at[2])
    get_neu = pltpu.make_async_copy(neu, nz.at[pl.ds(HERE, 1)], in_sem.at[3])
    my_rows = pl.ds(pl.multiple_of(me * 16, 16), 16)
    my_cols = pl.ds(pl.multiple_of(x * 512 + yh * 256, 256), 256)
    own_l = pltpu.make_async_copy(lad.at[0, :, my_cols], wl.at[my_rows], own_sem.at[0])
    own_c = pltpu.make_async_copy(cyc.at[0, :, my_cols], wc.at[my_rows], own_sem.at[1])
    get_amp.start()
    get_live.start()

    def at_z(k):
        return (e, x * 32 + yl * 16 + lax.rem(z + k + 16, 16))

    def member(k):
        pe = lax.rem(yh + 1 - lax.div(k, 8), 2) * 2 + lax.rem(
            co + 1 - lax.rem(lax.div(k, 4), 2), 2
        )
        px = lax.rem(x + 3 - lax.rem(k, 4), 4)
        return pe, px

    def near_z(k):
        return (4 - lax.div(k, 2)) * (1 - 2 * lax.rem(k, 2))

    bar = pltpu.get_barrier_semaphore()

    def greet(dev):
        pl.semaphore_signal(bar, inc=1, device_id=dev, device_id_type=MESH)

    @pl.loop(0, 8)
    def _(k):
        greet(at_z(near_z(k)))

    @pl.loop(0, 15)
    def _(k):
        pe, px = member(k)
        greet((pe, px * 32 + yl * 16 + z))

    @pl.loop(0, 4)
    def _(k):
        greet((k, x * 32 + (1 - yl) * 16 + z))

    @pl.loop(1, 4)
    def _(k):
        greet((e, lax.rem(x + k, 4) * 32 + (1 - yl) * 16 + z))

    get_neu.start()
    get_rec.start()
    own_l.start()
    own_c.start()

    order = lanes_by_half()
    get_live.wait()
    alive = jnp.where(r < live[e], 1.0, 0.0).astype(F32)
    get_amp.wait()
    block = mm((amp_v[...].astype(F32) * alive).astype(BF16), order)
    zbuf[HERE * 16 : HERE * 16 + 16, :] = block.astype(BF16)
    get_neu.wait()
    get_rec.wait()

    pl.semaphore_wait(bar, 30)

    def send(src, dst, ss, rs, dev):
        return pltpu.make_async_remote_copy(
            src_ref=src, dst_ref=dst, send_sem=ss, recv_sem=rs,
            device_id=dev, device_id_type=MESH,
        )

    def z_rows(slot):
        return pl.ds(pl.multiple_of(slot * 16, 16), 16)

    def z_copy(k, slot, to):
        lands = lax.rem(slot - to + 16, 16)
        return send(
            zbuf.at[z_rows(slot)], zbuf.at[z_rows(lands)], z_s.at[k], z_r.at[lands], at_z(to)
        )

    def n_copy(k, slot, to):
        lands = lax.rem(slot - to + 16, 16)
        return send(
            nz.at[pl.ds(slot, 1)], nz.at[pl.ds(lands, 1)], n_s.at[k], n_r.at[lands], at_z(to)
        )

    def z_wait(slot):
        here = zbuf.at[z_rows(slot)]
        send(here, here, z_s.at[0], z_r.at[slot], at_z(1)).wait_recv()

    def n_wait(slot):
        here = nz.at[pl.ds(slot, 1)]
        send(here, here, n_s.at[0], n_r.at[slot], at_z(1)).wait_recv()

    def relay_low(copy):
        @pl.loop(0, 4)
        def _(k):
            copy(8 + k, 0, 4 - k).start()

    def relay_high(copy):
        @pl.loop(0, 3)
        def _(k):
            copy(12 + k, 8, k - 3).start()

    @pl.loop(0, 8)
    def _(k):
        z_copy(k, HERE, near_z(k)).start()

    def n1_copy(k):
        g = lax.rem(group + k, 8)
        rows = nall.at[pl.ds(pl.multiple_of(group * 32, 32), 32)]
        dev = (e, lax.div(g, 2) * 32 + lax.rem(g, 2) * 16 + z)
        return send(rows, rows, n1_s.at[k], n1_r.at[group], dev)

    my_e = pl.ds(pl.multiple_of(e * 16, 16), 16)

    def s_copy(k):
        rows = sall.at[my_e]
        return send(rows, rows, s_s.at[k], s_r.at[e], (lax.rem(e + k, 4), r))

    def w_copy(src, dst, ss, rs, k):
        pe, px = member(k)
        cols = pl.ds(pl.multiple_of(px * 512 + lax.div(pe, 2) * 256, 256), 256)
        return send(
            src.at[0, :, cols], dst.at[my_rows], ss.at[k], rs.at[me],
            (pe, px * 32 + yl * 16 + z),
        )

    @pl.loop(0, 8)
    def _(k):
        n_copy(k, HERE, near_z(k)).start()

    @pl.loop(0, 15)
    def _(k):
        w_copy(lad, wl, wl_s, wl_r, k).start()
        w_copy(cyc, wc, wc_s, wc_r, k).start()

    sall[my_e, :] = swap_rows_lanes(block).astype(BF16)

    @pl.loop(1, 4)
    def _(k):
        s_copy(k).start()

    z_wait(0)
    relay_low(z_copy)
    z_wait(8)
    relay_high(z_copy)
    n_wait(0)
    relay_low(n_copy)
    n_wait(8)
    relay_high(n_copy)

    def a_copy(part, k):
        pco, pyl = lax.rem(k, 2), lax.div(k, 2)
        rows = pl.ds(0, NEAR * 16) if part == 0 else pl.ds(NEAR * 16, (SLOTS - NEAR) * 16)
        src = zbuf.at[rows, pl.ds(pl.multiple_of(pco * 128, 128), 128)]
        dst = abuf.at[rows, pl.ds(pl.multiple_of(e * 128, 128), 128)]
        dev = (yl * 2 + pco, x * 32 + pyl * 16 + z)
        return src, dst, a_s.at[part, k], a_r.at[part, e], dev

    def is_self(k):
        pco, pyl = lax.rem(k, 2), lax.div(k, 2)
        return jnp.logical_and(yh == yl, jnp.logical_and(pco == co, pyl == yl))

    def a_start(part):
        @pl.loop(0, 4)
        def _(k):
            src, dst, ss, rs, dev = a_copy(part, k)
            own = is_self(k)

            @pl.when(own)
            def _():
                pltpu.make_async_copy(src, dst, rs).start()

            @pl.when(jnp.logical_not(own))
            def _():
                send(src, dst, ss, rs, dev).start()

    def a_sent(part):
        @pl.loop(0, 4)
        def _(k):
            src, dst, ss, rs, dev = a_copy(part, k)

            @pl.when(jnp.logical_not(is_self(k)))
            def _():
                send(src, dst, ss, rs, dev).wait_send()

    def a_wait(part):
        rows = pl.ds(0, NEAR * 16) if part == 0 else pl.ds(NEAR * 16, (SLOTS - NEAR) * 16)

        @pl.loop(0, 4)
        def _(c):
            dst = abuf.at[rows, pl.ds(pl.multiple_of(c * 128, 128), 128)]
            send(dst, dst, a_s.at[0, 0], a_r.at[part, c], at_z(1)).wait_recv()

    def settle(first, last):
        value = abuf[first * 16 : last * 16, :]
        swapped = swap_rows_lanes(value.astype(F32)).astype(BF16)
        for slot in range(first, last):
            rows = pl.ds(pl.multiple_of(lax.rem(z + slot + 12, 16) * 16, 16), 16)
            at = (slot - first) * 16
            plain[rows, :] = value[at : at + 16]
            turned[rows, :] = swapped[at : at + 16]

    @pl.loop(1, 4)
    def _(k):
        z_wait(k)
        z_wait(k + 4)

    a_start(0)

    own_l.wait()
    own_c.wait()

    @pl.loop(0, 15)
    def _(k):
        pe, px = member(k)
        m = pe * 4 + px
        rows = pl.ds(pl.multiple_of(m * 16, 16), 16)
        send(wl.at[rows], wl.at[rows], wl_s.at[k], wl_r.at[m], at_z(1)).wait_recv()
        send(wc.at[rows], wc.at[rows], wc_s.at[k], wc_r.at[m], at_z(1)).wait_recv()

    @pl.loop(NEAR, SLOTS)
    def _(k):
        z_wait(k)

    a_start(1)

    a_wait(0)
    settle(0, NEAR)

    @pl.loop(1, 4)
    def _(k):
        n_wait(k)
        n_wait(k + 4)

    @pl.loop(NEAR, SLOTS)
    def _(k):
        n_wait(k)

    place = lax.broadcasted_iota(jnp.int32, (32, 256), 0)
    stacked = jnp.zeros((32, 256), F32)
    for slot in range(SLOTS):
        at = 2 * lax.rem(z + slot + 12, 16)
        pair = nz[slot].astype(F32)
        stacked = jnp.where(place == at, pair[0:1], stacked)
        stacked = jnp.where(place == at + 1, pair[1:2], stacked)
    nall[pl.ds(pl.multiple_of(group * 32, 32), 32), :] = stacked.astype(BF16)

    @pl.loop(1, 8)
    def _(k):
        n1_copy(k).start()

    a_wait(1)

    settle(NEAR, SLOTS)
    products = mm(wc[...], turned[...])
    for c in range(4):
        rows = slice(64 * c, 64 * c + 64)
        mixed = rec[c, 0] * products[rows, 0:128]
        for d in range(1, 4):
            mixed = mixed + rec[c, d] * products[rows, 128 * d : 128 * d + 128]
        fsend[rows, :] = swap_rows_lanes(mixed) + mm(
            wl[rows, :], plain[:, 128 * c : 128 * c + 128]
        )

    def f_copy(k):
        pe, px = member(k)
        rows = pl.ds(pl.multiple_of((pe * 4 + px) * 16, 16), 16)
        return send(
            fsend.at[rows], frecv.at[me], f_s.at[k], f_r.at[me],
            (pe, px * 32 + yl * 16 + z),
        )

    @pl.loop(0, 15)
    def _(k):
        f_copy(k).start()

    frecv[me] = fsend[my_rows, :]

    @pl.loop(1, 4)
    def _(k):
        c = lax.rem(e + k, 4)
        rows = sall.at[pl.ds(pl.multiple_of(c * 16, 16), 16)]
        send(rows, rows, s_s.at[k], s_r.at[c], at_z(1)).wait_recv()

    @pl.loop(1, 8)
    def _(k):
        g = lax.rem(group + k, 8)
        rows = nall.at[pl.ds(pl.multiple_of(g * 32, 32), 32)]
        send(rows, rows, n1_s.at[k], n1_r.at[g], at_z(1)).wait_recv()

    ordered = mm(neutron_row_order(), nall[...]).astype(BF16)
    ordered = mm(ordered, lanes_by_half()).astype(BF16)
    terms = lax.dot_general(
        sall[...], ordered, (((1,), (1,)), ((), ())), preferred_element_type=F32
    )
    neutron = rec[e, 0] * terms[0:16]
    for c in range(1, 4):
        neutron = neutron + rec[e, c] * terms[16 * c : 16 * c + 16]
    neutron = swap_rows_lanes(neutron)
    back = lanes_back()

    @pl.loop(0, 15)
    def _(k):
        pe, px = member(k)
        m = pe * 4 + px
        send(fsend.at[pl.ds(0, 16)], frecv.at[m], f_s.at[k], f_r.at[m], at_z(1)).wait_recv()

    halves = []
    for h in range(2):
        total = neutron[:, 128 * h : 128 * h + 128]
        for s in range(2):
            for i in range(4):
                total = total + frecv[(2 * s + h) * 4 + i]
        halves.append((total * alive).astype(BF16))
    out[0] = mm(jnp.concatenate(halves, axis=1), back).astype(BF16)

    @pl.loop(0, 8)
    def _(k):
        z_copy(k, HERE, near_z(k)).wait_send()
        n_copy(k, HERE, near_z(k)).wait_send()

    @pl.loop(8, 15)
    def _(k):
        z_copy(k, 0, 1).wait_send()
        n_copy(k, 0, 1).wait_send()

    for part in range(2):
        a_sent(part)

    @pl.loop(1, 8)
    def _(k):
        n1_copy(k).wait_send()

    @pl.loop(1, 4)
    def _(k):
        s_copy(k).wait_send()

    @pl.loop(0, 15)
    def _(k):
        w_copy(lad, wl, wl_s, wl_r, k).wait_send()
        w_copy(cyc, wc, wc_s, wc_r, k).wait_send()
        f_copy(k).wait_send()


def local(amplitudes, ladder_pp, cycle_proton, cycle_neutron, recouple, proton_live):
    dma = pltpu.SemaphoreType.DMA
    operands = (amplitudes, ladder_pp, cycle_proton, cycle_neutron, recouple, proton_live)
    return pl.pallas_call(
        kernel,
        out_shape=pltpu.VMEM((1, 16, 256), BF16),
        in_specs=[pl.BlockSpec(memory_space=pltpu.HBM)] * 6,
        out_specs=pl.BlockSpec(memory_space=pltpu.VMEM),
        scratch_shapes=[
            pltpu.SMEM((4, 4), F32),
            pltpu.SMEM((4,), jnp.int32),
            pltpu.VMEM((16, 256), BF16),
            pltpu.VMEM((256, 256), BF16),
            pltpu.VMEM((16, 2, 256), BF16),
            pltpu.VMEM((64, 256), BF16),
            pltpu.VMEM((256, 256), BF16),
            pltpu.VMEM((256, 256), BF16),
            pltpu.VMEM((256, 256), BF16),
            pltpu.VMEM((256, 512), BF16),
            pltpu.VMEM((256, 512), BF16),
            pltpu.VMEM((256, 512), BF16),
            pltpu.VMEM((256, 128), F32),
            pltpu.VMEM((16, 16, 128), F32),
            dma((4,)),
            dma((2,)),
            dma((15,)),
            dma((16,)),
            dma((15,)),
            dma((16,)),
            dma((4,)),
            dma((4,)),
            dma((8,)),
            dma((8,)),
            dma((15,)),
            dma((16,)),
            dma((15,)),
            dma((16,)),
            dma((2, 4)),
            dma((2, 4)),
            dma((15,)),
            dma((16,)),
        ],
        compiler_params=pltpu.CompilerParams(
            collective_id=0, has_side_effects=True, vmem_limit_bytes=16 << 20
        ),
        name="pair_residual",
    )(*(pltpu.with_memory_space_constraint(v, pltpu.HBM) for v in operands))


def solution(mesh):
    rows = P("chan", "row", None)
    return jax.shard_map(
        local,
        mesh=mesh,
        in_specs=(rows, rows, rows, rows, P(), P()),
        out_specs=rows,
        check_vma=False,
    )
```

time: 44.4 us -> 37.2 us (0.84)
  local copies, waits for them, and re-layouts: 4.99 us -> 0.6 us
  Pallas kernels: 39.1 us -> 36.4 us
    unnamed x13 -> x1, local copies, waits for them, and re-layouts: 4.99 us -> 0.6 us
    pallas_call x1, Pallas kernels: 39.1 us -> 36.4 us  [local(): pl.pallas_call(kernel, out_shape=pltpu.VMEM((1, 16, 256), BF16), in_specs...]
where the time goes in v2:
time: 37.2 us; the launch traced here: 37 us
  Pallas kernels  36.4 us (98%)
  local copies, waits for them, and re-layouts  0.6 us (2%)
    pallas_call x1, Pallas kernels, local(): pl.pallas_call(kernel, out_shape=pltpu.VMEM((1, 16, 256), BF16), in_specs...  36.4 us

profile of v2, /device:TPU:1, one launch (start us, length us, event | category | flops | bytes accessed | tf_op | source)
XLA Modules:
  0.0 37.0 jit_solution(12111352604282890150)
XLA Ops:
  0.0 36.4 %pair_residual.1 = bf16[1,16,256]{2,1,0:T(8,128)(2,1)S(1)} custom-call(bf16[1,16,256]{2,1,0:T(8,128)(2,1)} %amp.1, bf16[1,16,2048]{2,1,0:T(8,128)(2,1)} %lad.1, bf16[1,16,2048]{2,1,0:T(8,128)(2,1)} %cyc.1, bf16[1,2,256]{2,1,0:T(2,128)(2,1)} %neu.1, f32[4,4]{1,0:T(4,128)} %rec_in.1, s32[4]{0:T(128)} %live_in.1), custom_call_target="tpu_custom_call" | custom-call | tf_op jit(solution)/shard_map/pair_residual/pallas_call | solution.py:423
  36.4 0.6 %copy.8 = bf16[1,16,256]{2,1,0:T(8,128)(2,1)} copy(bf16[1,16,256]{2,1,0:T(8,128)(2,1)S(1)} %pair_residual.1) | data formatting | bytes 16384

commit v3 on v2

--- a/solution.py
+++ b/solution.py
@@ -54,17 +54,26 @@
     return jnp.where(goes == new, 1.0, 0.0).astype(BF16)
 
 
+def div(a, b):
+    return a // b if isinstance(a, int) else lax.div(a, b)
+
+
+def rem(a, b):
+    return a % b if isinstance(a, int) else lax.rem(a, b)
+
+
 def mm(a, b):
     return jnp.dot(a, b, preferred_element_type=F32)
 
 
 NEAR, SLOTS = 9, 16
+LATE, EARLY = 8, 2
 HERE = 4
 
 
 def kernel(
     amp, lad, cyc, neu, rec_in, live_in, out,
-    rec, live, amp_v, zbuf, nz, sall, nall, wl, wc, abuf, plain, turned, fsend, frecv,
+    rec, live, amp_v, zbuf, nz, sall, nall, wl, wc, abuf, plain, turned, orders, fsend, frecv,
     in_sem, own_sem, z_s, z_r, n_s, n_r, s_s, s_r, n1_s, n1_r,
     wl_s, wl_r, wc_s, wc_r, a_s, a_r, f_s, f_r,
 ):
@@ -79,45 +88,51 @@
     get_rec = pltpu.make_async_copy(rec_in, rec, in_sem.at[2])
     get_neu = pltpu.make_async_copy(neu, nz.at[pl.ds(HERE, 1)], in_sem.at[3])
     my_rows = pl.ds(pl.multiple_of(me * 16, 16), 16)
-    my_cols = pl.ds(pl.multiple_of(x * 512 + yh * 256, 256), 256)
+    my_cols = pl.ds(pl.multiple_of(x * 512 + co * 256, 256), 256)
     own_l = pltpu.make_async_copy(lad.at[0, :, my_cols], wl.at[my_rows], own_sem.at[0])
     own_c = pltpu.make_async_copy(cyc.at[0, :, my_cols], wc.at[my_rows], own_sem.at[1])
     get_amp.start()
     get_live.start()
 
     def at_z(k):
-        return (e, x * 32 + yl * 16 + lax.rem(z + k + 16, 16))
+        return (e, x * 32 + yl * 16 + lax.rem(z + k + 32, 16))
 
     def member(k):
-        pe = lax.rem(yh + 1 - lax.div(k, 8), 2) * 2 + lax.rem(
-            co + 1 - lax.rem(lax.div(k, 4), 2), 2
-        )
-        px = lax.rem(x + 3 - lax.rem(k, 4), 4)
+        pe = rem(yh + 1 - div(k, 8), 2) * 2 + rem(co + 1 - rem(div(k, 4), 2), 2)
+        px = rem(x + 3 - rem(k, 4), 4)
         return pe, px
 
     def near_z(k):
-        return (4 - lax.div(k, 2)) * (1 - 2 * lax.rem(k, 2))
+        return (4 - div(k, 2)) * (1 - 2 * rem(k, 2))
 
     bar = pltpu.get_barrier_semaphore()
 
     def greet(dev):
         pl.semaphore_signal(bar, inc=1, device_id=dev, device_id_type=MESH)
 
-    @pl.loop(0, 8)
-    def _(k):
-        greet(at_z(near_z(k)))
-
-    @pl.loop(0, 15)
-    def _(k):
+    for k in (1, 5, 0, 2, 4, 6, 9, 13):
         pe, px = member(k)
         greet((pe, px * 32 + yl * 16 + z))
-
-    @pl.loop(0, 4)
-    def _(k):
+        greet(at_z(near_z((1, 5, 0, 2, 4, 6, 9, 13).index(k))))
+    for k in (3, 7, 8, 10, 11, 12, 14):
+        pe, px = member(k)
+        greet((pe, px * 32 + yl * 16 + z))
+
+    def apart(p, q):
+        ahead = lax.rem(p - q + 16, 16)
+        return jnp.minimum(ahead, 16 - ahead)
+
+    @pl.when(z < EARLY)
+    def _():
+        @pl.loop(LATE, 16)
+        def _(s):
+            @pl.when(apart(s, z) > 4)
+            def _():
+                greet((e, x * 32 + yl * 16 + s))
+
+    for k in range(4):
         greet((k, x * 32 + (1 - yl) * 16 + z))
-
-    @pl.loop(1, 4)
-    def _(k):
+    for k in range(1, 4):
         greet((e, lax.rem(x + k, 4) * 32 + (1 - yl) * 16 + z))
 
     get_neu.start()
@@ -134,7 +149,10 @@
     get_neu.wait()
     get_rec.wait()
 
-    pl.semaphore_wait(bar, 30)
+    straight = 0
+    for d in range(EARLY):
+        straight = straight + jnp.where(apart(z, d) > 4, 1, 0)
+    pl.semaphore_wait(bar, 30 + jnp.where(z >= LATE, straight, 0))
 
     def send(src, dst, ss, rs, dev):
         return pltpu.make_async_remote_copy(
@@ -146,13 +164,13 @@
         return pl.ds(pl.multiple_of(slot * 16, 16), 16)
 
     def z_copy(k, slot, to):
-        lands = lax.rem(slot - to + 16, 16)
+        lands = rem(slot - to + 32, 16)
         return send(
             zbuf.at[z_rows(slot)], zbuf.at[z_rows(lands)], z_s.at[k], z_r.at[lands], at_z(to)
         )
 
     def n_copy(k, slot, to):
-        lands = lax.rem(slot - to + 16, 16)
+        lands = rem(slot - to + 32, 16)
         return send(
             nz.at[pl.ds(slot, 1)], nz.at[pl.ds(lands, 1)], n_s.at[k], n_r.at[lands], at_z(to)
         )
@@ -165,18 +183,48 @@
         here = nz.at[pl.ds(slot, 1)]
         send(here, here, n_s.at[0], n_r.at[slot], at_z(1)).wait_recv()
 
-    def relay_low(copy):
+    def goes_straight(source, to):
+        return jnp.logical_and(
+            lax.rem(z + source + 16, 16) >= LATE, lax.rem(z + to + 16, 16) < EARLY
+        )
+
+    def each_straight(act):
+        @pl.when(z >= LATE)
+        def _():
+            @pl.loop(0, EARLY)
+            def _(d):
+                @pl.when(apart(z, d) > 4)
+                def _():
+                    act(15 + d, HERE, d - z)
+
+    def each_low(act):
         @pl.loop(0, 4)
         def _(k):
-            copy(8 + k, 0, 4 - k).start()
-
-    def relay_high(copy):
+            @pl.when(jnp.logical_not(goes_straight(-4, 4 - k)))
+            def _():
+                act(8 + k, 0, 4 - k)
+
+    def each_high(act):
         @pl.loop(0, 3)
         def _(k):
-            copy(12 + k, 8, k - 3).start()
-
-    @pl.loop(0, 8)
-    def _(k):
+            @pl.when(jnp.logical_not(goes_straight(4, k - 3)))
+            def _():
+                act(12 + k, 8, k - 3)
+
+    def z_start(k, slot, to):
+        z_copy(k, slot, to).start()
+
+    def n_start(k, slot, to):
+        n_copy(k, slot, to).start()
+
+    def z_sent(k, slot, to):
+        z_copy(k, slot, to).wait_send()
+
+    def n_sent(k, slot, to):
+        n_copy(k, slot, to).wait_send()
+
+    each_straight(z_start)
+    for k in range(8):
         z_copy(k, HERE, near_z(k)).start()
 
     def n1_copy(k):
@@ -193,20 +241,40 @@
 
     def w_copy(src, dst, ss, rs, k):
         pe, px = member(k)
-        cols = pl.ds(pl.multiple_of(px * 512 + lax.div(pe, 2) * 256, 256), 256)
+        cols = pl.ds(pl.multiple_of(px * 512 + lax.rem(pe, 2) * 256, 256), 256)
         return send(
             src.at[0, :, cols], dst.at[my_rows], ss.at[k], rs.at[me],
             (pe, px * 32 + yl * 16 + z),
         )
 
+    each_straight(n_start)
+
     @pl.loop(0, 8)
     def _(k):
         n_copy(k, HERE, near_z(k)).start()
 
-    @pl.loop(0, 15)
-    def _(k):
-        w_copy(lad, wl, wl_s, wl_r, k).start()
-        w_copy(cyc, wc, wc_s, wc_r, k).start()
+    def weights_out():
+        @pl.loop(0, 15)
+        def _(k):
+            w_copy(lad, wl, wl_s, wl_r, k).start()
+            w_copy(cyc, wc, wc_s, wc_r, k).start()
+
+    @pl.when(z < LATE)
+    def _():
+        weights_out()
+
+    z_wait(0)
+    each_low(z_start)
+    z_wait(8)
+    each_high(z_start)
+    n_wait(0)
+    each_low(n_start)
+    n_wait(8)
+    each_high(n_start)
+
+    @pl.when(z >= LATE)
+    def _():
+        weights_out()
 
     sall[my_e, :] = swap_rows_lanes(block).astype(BF16)
 
@@ -214,26 +282,20 @@
     def _(k):
         s_copy(k).start()
 
-    z_wait(0)
-    relay_low(z_copy)
-    z_wait(8)
-    relay_high(z_copy)
-    n_wait(0)
-    relay_low(n_copy)
-    n_wait(8)
-    relay_high(n_copy)
+    def away_y(k):
+        y = lax.rem(yh * 2 + yl + lax.rem(k + 2, 4) + lax.div(k, 2) * (5 - 2 * k), 4)
+        return lax.div(y, 2), lax.rem(y, 2)
 
     def a_copy(part, k):
-        pco, pyl = lax.rem(k, 2), lax.div(k, 2)
+        pyh, pyl = away_y(k)
         rows = pl.ds(0, NEAR * 16) if part == 0 else pl.ds(NEAR * 16, (SLOTS - NEAR) * 16)
-        src = zbuf.at[rows, pl.ds(pl.multiple_of(pco * 128, 128), 128)]
+        src = zbuf.at[rows, pl.ds(pl.multiple_of(pyh * 128, 128), 128)]
         dst = abuf.at[rows, pl.ds(pl.multiple_of(e * 128, 128), 128)]
-        dev = (yl * 2 + pco, x * 32 + pyl * 16 + z)
+        dev = (pyh * 2 + yl, x * 32 + pyl * 16 + z)
         return src, dst, a_s.at[part, k], a_r.at[part, e], dev
 
     def is_self(k):
-        pco, pyl = lax.rem(k, 2), lax.div(k, 2)
-        return jnp.logical_and(yh == yl, jnp.logical_and(pco == co, pyl == yl))
+        return jnp.logical_and(co == yl, k == 3)
 
     def a_start(part):
         @pl.loop(0, 4)
@@ -275,6 +337,10 @@
             plain[rows, :] = value[at : at + 16]
             turned[rows, :] = swapped[at : at + 16]
 
+    orders[0] = order
+    orders[1] = lanes_back()
+    orders[2] = neutron_row_order()
+
     @pl.loop(1, 4)
     def _(k):
         z_wait(k)
@@ -298,9 +364,6 @@
         z_wait(k)
 
     a_start(1)
-
-    a_wait(0)
-    settle(0, NEAR)
 
     @pl.loop(1, 4)
     def _(k):
@@ -323,6 +386,9 @@
     @pl.loop(1, 8)
     def _(k):
         n1_copy(k).start()
+
+    a_wait(0)
+    settle(0, NEAR)
 
     a_wait(1)
 
@@ -345,8 +411,7 @@
             (pe, px * 32 + yl * 16 + z),
         )
 
-    @pl.loop(0, 15)
-    def _(k):
+    for k in (1, 5, 0, 2, 4, 6, 9, 13, 3, 7, 8, 10, 11, 12, 14):
         f_copy(k).start()
 
     frecv[me] = fsend[my_rows, :]
@@ -363,8 +428,8 @@
         rows = nall.at[pl.ds(pl.multiple_of(g * 32, 32), 32)]
         send(rows, rows, n1_s.at[k], n1_r.at[g], at_z(1)).wait_recv()
 
-    ordered = mm(neutron_row_order(), nall[...]).astype(BF16)
-    ordered = mm(ordered, lanes_by_half()).astype(BF16)
+    ordered = mm(orders[2], nall[...]).astype(BF16)
+    ordered = mm(ordered, orders[0]).astype(BF16)
     terms = lax.dot_general(
         sall[...], ordered, (((1,), (1,)), ((), ())), preferred_element_type=F32
     )
@@ -372,7 +437,33 @@
     for c in range(1, 4):
         neutron = neutron + rec[e, c] * terms[16 * c : 16 * c + 16]
     neutron = swap_rows_lanes(neutron)
-    back = lanes_back()
+
+    @pl.loop(0, 8)
+    def _(k):
+        z_copy(k, HERE, near_z(k)).wait_send()
+        n_copy(k, HERE, near_z(k)).wait_send()
+
+    for sent in (z_sent, n_sent):
+        each_straight(sent)
+        each_low(sent)
+        each_high(sent)
+
+    for part in range(2):
+        a_sent(part)
+
+    @pl.loop(1, 8)
+    def _(k):
+        n1_copy(k).wait_send()
+
+    @pl.loop(1, 4)
+    def _(k):
+        s_copy(k).wait_send()
+
+    @pl.loop(0, 15)
+    def _(k):
+        w_copy(lad, wl, wl_s, wl_r, k).wait_send()
+        w_copy(cyc, wc, wc_s, wc_r, k).wait_send()
+        f_copy(k).wait_send()
 
     @pl.loop(0, 15)
     def _(k):
@@ -385,36 +476,9 @@
         total = neutron[:, 128 * h : 128 * h + 128]
         for s in range(2):
             for i in range(4):
-                total = total + frecv[(2 * s + h) * 4 + i]
+                total = total + frecv[(2 * h + s) * 4 + i]
         halves.append((total * alive).astype(BF16))
-    out[0] = mm(jnp.concatenate(halves, axis=1), back).astype(BF16)
-
-    @pl.loop(0, 8)
-    def _(k):
-        z_copy(k, HERE, near_z(k)).wait_send()
-        n_copy(k, HERE, near_z(k)).wait_send()
-
-    @pl.loop(8, 15)
-    def _(k):
-        z_copy(k, 0, 1).wait_send()
-        n_copy(k, 0, 1).wait_send()
-
-    for part in range(2):
-        a_sent(part)
-
-    @pl.loop(1, 8)
-    def _(k):
-        n1_copy(k).wait_send()
-
-    @pl.loop(1, 4)
-    def _(k):
-        s_copy(k).wait_send()
-
-    @pl.loop(0, 15)
-    def _(k):
-        w_copy(lad, wl, wl_s, wl_r, k).wait_send()
-        w_copy(cyc, wc, wc_s, wc_r, k).wait_send()
-        f_copy(k).wait_send()
+    out[0] = mm(jnp.concatenate(halves, axis=1), orders[1]).astype(BF16)
 
 
 def local(amplitudes, ladder_pp, cycle_proton, cycle_neutron, recouple, proton_live):
@@ -438,13 +502,14 @@
             pltpu.VMEM((256, 512), BF16),
             pltpu.VMEM((256, 512), BF16),
             pltpu.VMEM((256, 512), BF16),
+            pltpu.VMEM((3, 256, 256), BF16),
             pltpu.VMEM((256, 128), F32),
             pltpu.VMEM((16, 16, 128), F32),
             dma((4,)),
             dma((2,)),
-            dma((15,)),
+            dma((15 + EARLY,)),
             dma((16,)),
-            dma((15,)),
+            dma((15 + EARLY,)),
             dma((16,)),
             dma((4,)),
             dma((4,)),

time: 37.2 us -> 35.8 us (0.962)
  Pallas kernels: 36.4 us -> 35 us
    pallas_call x1, Pallas kernels: 36.4 us -> 35 us  [local(): pl.pallas_call(kernel, out_shape=pltpu.VMEM((1, 16, 256), BF16), in_specs...]
where the time goes in v3:
time: 35.8 us; the launch traced here: 35.6 us
  Pallas kernels  35 us (98%)
  local copies, waits for them, and re-layouts  0.6 us (2%)
    pallas_call x1, Pallas kernels, local(): pl.pallas_call(kernel, out_shape=pltpu.VMEM((1, 16, 256), BF16), in_specs...  35 us

profile of v3, /device:TPU:1, one launch (start us, length us, event | category | flops | bytes accessed | tf_op | source)
XLA Modules:
  0.0 35.6 jit_solution(8974402993598437643)
XLA Ops:
  0.0 35.0 %pair_residual.1 = bf16[1,16,256]{2,1,0:T(8,128)(2,1)S(1)} custom-call(bf16[1,16,256]{2,1,0:T(8,128)(2,1)} %amp.1, bf16[1,16,2048]{2,1,0:T(8,128)(2,1)} %lad.1, bf16[1,16,2048]{2,1,0:T(8,128)(2,1)} %cyc.1, bf16[1,2,256]{2,1,0:T(2,128)(2,1)} %neu.1, f32[4,4]{1,0:T(4,128)} %rec_in.1, s32[4]{0:T(128)} %live_in.1), custom_call_target="tpu_custom_call" | custom-call | tf_op jit(solution)/shard_map/pair_residual/pallas_call | solution.py:487
  35.0 0.6 %copy.8 = bf16[1,16,256]{2,1,0:T(8,128)(2,1)} copy(bf16[1,16,256]{2,1,0:T(8,128)(2,1)S(1)} %pair_residual.1) | data formatting | bytes 16384

commit v4 on v3

--- a/solution.py
+++ b/solution.py
@@ -66,16 +66,17 @@
     return jnp.dot(a, b, preferred_element_type=F32)
 
 
-NEAR, SLOTS = 9, 16
+SLOTS = 16
+PARTS = ((4, 9), (0, 4), (9, 12), (12, 16))
 LATE, EARLY = 8, 2
 HERE = 4
 
 
 def kernel(
     amp, lad, cyc, neu, rec_in, live_in, out,
-    rec, live, amp_v, zbuf, nz, sall, nall, wl, wc, abuf, plain, turned, orders, fsend, frecv,
-    in_sem, own_sem, z_s, z_r, n_s, n_r, s_s, s_r, n1_s, n1_r,
-    wl_s, wl_r, wc_s, wc_r, a_s, a_r, f_s, f_r,
+    rec, live, amp_v, zbuf, nz, sall, nall, wts, abuf, plain, turned, orders, fsend, frecv,
+    in_sem, z_s, z_r, n_s, n_r, s_s, s_r, n1_s, n1_r,
+    w_s, w_r, a_s, a_r, f_s, f_r,
 ):
     e, r = lax.axis_index("chan"), lax.axis_index("row")
     yh, co = lax.div(e, 2), lax.rem(e, 2)
@@ -88,9 +89,10 @@
     get_rec = pltpu.make_async_copy(rec_in, rec, in_sem.at[2])
     get_neu = pltpu.make_async_copy(neu, nz.at[pl.ds(HERE, 1)], in_sem.at[3])
     my_rows = pl.ds(pl.multiple_of(me * 16, 16), 16)
+    low_rows = pl.ds(pl.multiple_of(256 + me * 16, 16), 16)
     my_cols = pl.ds(pl.multiple_of(x * 512 + co * 256, 256), 256)
-    own_l = pltpu.make_async_copy(lad.at[0, :, my_cols], wl.at[my_rows], own_sem.at[0])
-    own_c = pltpu.make_async_copy(cyc.at[0, :, my_cols], wc.at[my_rows], own_sem.at[1])
+    own_l = pltpu.make_async_copy(lad.at[0, :, my_cols], wts.at[my_rows], w_r)
+    own_c = pltpu.make_async_copy(cyc.at[0, :, my_cols], wts.at[low_rows], w_r)
     get_amp.start()
     get_live.start()
 
@@ -146,8 +148,6 @@
     get_amp.wait()
     block = mm((amp_v[...].astype(F32) * alive).astype(BF16), order)
     zbuf[HERE * 16 : HERE * 16 + 16, :] = block.astype(BF16)
-    get_neu.wait()
-    get_rec.wait()
 
     straight = 0
     for d in range(EARLY):
@@ -231,22 +231,29 @@
         g = lax.rem(group + k, 8)
         rows = nall.at[pl.ds(pl.multiple_of(group * 32, 32), 32)]
         dev = (e, lax.div(g, 2) * 32 + lax.rem(g, 2) * 16 + z)
-        return send(rows, rows, n1_s.at[k], n1_r.at[group], dev)
+        return send(rows, rows, n1_s, n1_r, dev)
 
     my_e = pl.ds(pl.multiple_of(e * 16, 16), 16)
 
     def s_copy(k):
         rows = sall.at[my_e]
-        return send(rows, rows, s_s.at[k], s_r.at[e], (lax.rem(e + k, 4), r))
-
-    def w_copy(src, dst, ss, rs, k):
+        return send(rows, rows, s_s, s_r, (lax.rem(e + k, 4), r))
+
+    def w_copy(src, rows, k):
         pe, px = member(k)
         cols = pl.ds(pl.multiple_of(px * 512 + lax.rem(pe, 2) * 256, 256), 256)
         return send(
-            src.at[0, :, cols], dst.at[my_rows], ss.at[k], rs.at[me],
-            (pe, px * 32 + yl * 16 + z),
-        )
-
+            src.at[0, :, cols], wts.at[rows], w_s, w_r, (pe, px * 32 + yl * 16 + z)
+        )
+
+    def all_here(ref, sem):
+        send(ref, ref, sem, sem, at_z(1)).wait_recv()
+
+    def all_gone(ref, sem):
+        send(ref, ref, sem, sem, at_z(1)).wait_send()
+
+    get_neu.wait()
+    get_rec.wait()
     each_straight(n_start)
 
     @pl.loop(0, 8)
@@ -256,39 +263,24 @@
     def weights_out():
         @pl.loop(0, 15)
         def _(k):
-            w_copy(lad, wl, wl_s, wl_r, k).start()
-            w_copy(cyc, wc, wc_s, wc_r, k).start()
+            w_copy(lad, my_rows, k).start()
+            w_copy(cyc, low_rows, k).start()
 
     @pl.when(z < LATE)
     def _():
         weights_out()
 
-    z_wait(0)
-    each_low(z_start)
-    z_wait(8)
-    each_high(z_start)
-    n_wait(0)
-    each_low(n_start)
-    n_wait(8)
-    each_high(n_start)
-
-    @pl.when(z >= LATE)
-    def _():
-        weights_out()
-
-    sall[my_e, :] = swap_rows_lanes(block).astype(BF16)
-
-    @pl.loop(1, 4)
-    def _(k):
-        s_copy(k).start()
-
     def away_y(k):
         y = lax.rem(yh * 2 + yl + lax.rem(k + 2, 4) + lax.div(k, 2) * (5 - 2 * k), 4)
         return lax.div(y, 2), lax.rem(y, 2)
 
+    def part_rows(part):
+        first, last = PARTS[part]
+        return pl.ds(first * 16, (last - first) * 16)
+
     def a_copy(part, k):
         pyh, pyl = away_y(k)
-        rows = pl.ds(0, NEAR * 16) if part == 0 else pl.ds(NEAR * 16, (SLOTS - NEAR) * 16)
+        rows = part_rows(part)
         src = zbuf.at[rows, pl.ds(pl.multiple_of(pyh * 128, 128), 128)]
         dst = abuf.at[rows, pl.ds(pl.multiple_of(e * 128, 128), 128)]
         dev = (pyh * 2 + yl, x * 32 + pyl * 16 + z)
@@ -321,12 +313,36 @@
                 send(src, dst, ss, rs, dev).wait_send()
 
     def a_wait(part):
-        rows = pl.ds(0, NEAR * 16) if part == 0 else pl.ds(NEAR * 16, (SLOTS - NEAR) * 16)
+        rows = part_rows(part)
 
         @pl.loop(0, 4)
         def _(c):
             dst = abuf.at[rows, pl.ds(pl.multiple_of(c * 128, 128), 128)]
             send(dst, dst, a_s.at[0, 0], a_r.at[part, c], at_z(1)).wait_recv()
+
+    for slot in (5, 6, 7, 8):
+        z_wait(slot)
+    each_high(z_start)
+    a_start(0)
+    z_wait(0)
+    each_low(z_start)
+    for slot in (1, 2, 3):
+        z_wait(slot)
+    a_start(1)
+    n_wait(0)
+    each_low(n_start)
+    n_wait(8)
+    each_high(n_start)
+
+    @pl.when(z >= LATE)
+    def _():
+        weights_out()
+
+    sall[my_e, :] = swap_rows_lanes(block).astype(BF16)
+
+    @pl.loop(1, 4)
+    def _(k):
+        s_copy(k).start()
 
     def settle(first, last):
         value = abuf[first * 16 : last * 16, :]
@@ -341,36 +357,31 @@
     orders[1] = lanes_back()
     orders[2] = neutron_row_order()
 
-    @pl.loop(1, 4)
+    all_here(wts, w_r)
+
+    all_gone(sall.at[0:48], s_s)
+    all_gone(wts.at[0:480], w_s)
+
+    @pl.loop(0, 8)
     def _(k):
-        z_wait(k)
-        z_wait(k + 4)
-
-    a_start(0)
-
-    own_l.wait()
-    own_c.wait()
-
-    @pl.loop(0, 15)
-    def _(k):
-        pe, px = member(k)
-        m = pe * 4 + px
-        rows = pl.ds(pl.multiple_of(m * 16, 16), 16)
-        send(wl.at[rows], wl.at[rows], wl_s.at[k], wl_r.at[m], at_z(1)).wait_recv()
-        send(wc.at[rows], wc.at[rows], wc_s.at[k], wc_r.at[m], at_z(1)).wait_recv()
-
-    @pl.loop(NEAR, SLOTS)
-    def _(k):
-        z_wait(k)
-
-    a_start(1)
+        z_copy(k, HERE, near_z(k)).wait_send()
+        n_copy(k, HERE, near_z(k)).wait_send()
+
+    for part in (2, 3):
+        for slot in range(*PARTS[part]):
+            z_wait(slot)
+        a_start(part)
+
+    a_wait(0)
+    a_wait(1)
+    settle(0, 9)
 
     @pl.loop(1, 4)
     def _(k):
         n_wait(k)
         n_wait(k + 4)
 
-    @pl.loop(NEAR, SLOTS)
+    @pl.loop(9, SLOTS)
     def _(k):
         n_wait(k)
 
@@ -387,27 +398,31 @@
     def _(k):
         n1_copy(k).start()
 
-    a_wait(0)
-    settle(0, NEAR)
-
-    a_wait(1)
-
-    settle(NEAR, SLOTS)
-    products = mm(wc[...], turned[...])
+    for sent in (z_sent, n_sent):
+        each_straight(sent)
+        each_low(sent)
+        each_high(sent)
+
+    a_wait(2)
+    settle(9, 12)
+    a_wait(3)
+
+    settle(12, 16)
+    products = mm(wts[256:512, :], turned[...])
     for c in range(4):
         rows = slice(64 * c, 64 * c + 64)
         mixed = rec[c, 0] * products[rows, 0:128]
         for d in range(1, 4):
             mixed = mixed + rec[c, d] * products[rows, 128 * d : 128 * d + 128]
         fsend[rows, :] = swap_rows_lanes(mixed) + mm(
-            wl[rows, :], plain[:, 128 * c : 128 * c + 128]
+            wts[rows, :], plain[:, 128 * c : 128 * c + 128]
         )
 
     def f_copy(k):
         pe, px = member(k)
         rows = pl.ds(pl.multiple_of((pe * 4 + px) * 16, 16), 16)
         return send(
-            fsend.at[rows], frecv.at[me], f_s.at[k], f_r.at[me],
+            fsend.at[rows], frecv.at[me], f_s, f_r,
             (pe, px * 32 + yl * 16 + z),
         )
 
@@ -416,17 +431,8 @@
 
     frecv[me] = fsend[my_rows, :]
 
-    @pl.loop(1, 4)
-    def _(k):
-        c = lax.rem(e + k, 4)
-        rows = sall.at[pl.ds(pl.multiple_of(c * 16, 16), 16)]
-        send(rows, rows, s_s.at[k], s_r.at[c], at_z(1)).wait_recv()
-
-    @pl.loop(1, 8)
-    def _(k):
-        g = lax.rem(group + k, 8)
-        rows = nall.at[pl.ds(pl.multiple_of(g * 32, 32), 32)]
-        send(rows, rows, n1_s.at[k], n1_r.at[g], at_z(1)).wait_recv()
+    all_here(sall.at[0:48], s_r)
+    all_here(nall.at[0:224], n1_r)
 
     ordered = mm(orders[2], nall[...]).astype(BF16)
     ordered = mm(ordered, orders[0]).astype(BF16)
@@ -438,38 +444,13 @@
         neutron = neutron + rec[e, c] * terms[16 * c : 16 * c + 16]
     neutron = swap_rows_lanes(neutron)
 
-    @pl.loop(0, 8)
-    def _(k):
-        z_copy(k, HERE, near_z(k)).wait_send()
-        n_copy(k, HERE, near_z(k)).wait_send()
-
-    for sent in (z_sent, n_sent):
-        each_straight(sent)
-        each_low(sent)
-        each_high(sent)
-
-    for part in range(2):
+    for part in range(4):
         a_sent(part)
 
-    @pl.loop(1, 8)
-    def _(k):
-        n1_copy(k).wait_send()
-
-    @pl.loop(1, 4)
-    def _(k):
-        s_copy(k).wait_send()
-
-    @pl.loop(0, 15)
-    def _(k):
-        w_copy(lad, wl, wl_s, wl_r, k).wait_send()
-        w_copy(cyc, wc, wc_s, wc_r, k).wait_send()
-        f_copy(k).wait_send()
-
-    @pl.loop(0, 15)
-    def _(k):
-        pe, px = member(k)
-        m = pe * 4 + px
-        send(fsend.at[pl.ds(0, 16)], frecv.at[m], f_s.at[k], f_r.at[m], at_z(1)).wait_recv()
+    all_gone(nall.at[0:224], n1_s)
+    all_gone(fsend.at[0:240], f_s)
+
+    all_here(frecv.at[0:15], f_r)
 
     halves = []
     for h in range(2):
@@ -497,8 +478,7 @@
             pltpu.VMEM((16, 2, 256), BF16),
             pltpu.VMEM((64, 256), BF16),
             pltpu.VMEM((256, 256), BF16),
-            pltpu.VMEM((256, 256), BF16),
-            pltpu.VMEM((256, 256), BF16),
+            pltpu.VMEM((512, 256), BF16),
             pltpu.VMEM((256, 512), BF16),
             pltpu.VMEM((256, 512), BF16),
             pltpu.VMEM((256, 512), BF16),
@@ -506,23 +486,20 @@
             pltpu.VMEM((256, 128), F32),
             pltpu.VMEM((16, 16, 128), F32),
             dma((4,)),
-            dma((2,)),
             dma((15 + EARLY,)),
             dma((16,)),
             dma((15 + EARLY,)),
             dma((16,)),
-            dma((4,)),
-            dma((4,)),
-            dma((8,)),
-            dma((8,)),
-            dma((15,)),
-            dma((16,)),
-            dma((15,)),
-            dma((16,)),
-            dma((2, 4)),
-            dma((2, 4)),
-            dma((15,)),
-            dma((16,)),
+            dma,
+            dma,
+            dma,
+            dma,
+            dma,
+            dma,
+            dma((4, 4)),
+            dma((4, 4)),
+            dma,
+            dma,
         ],
         compiler_params=pltpu.CompilerParams(
             collective_id=0, has_side_effects=True, vmem_limit_bytes=16 << 20

time: 35.8 us -> 34.8 us (0.972)
  Pallas kernels: 35 us -> 34 us
    pallas_call x1, Pallas kernels: 35 us -> 34 us  [local(): pl.pallas_call(kernel, out_shape=pltpu.VMEM((1, 16, 256), BF16), in_specs...]
where the time goes in v4:
time: 34.8 us; the launch traced here: 34.6 us
  Pallas kernels  34 us (98%)
  local copies, waits for them, and re-layouts  0.6 us (2%)
    pallas_call x1, Pallas kernels, local(): pl.pallas_call(kernel, out_shape=pltpu.VMEM((1, 16, 256), BF16), in_specs...  34 us

profile of v4, /device:TPU:1, one launch (start us, length us, event | category | flops | bytes accessed | tf_op | source)
XLA Modules:
  0.0 34.6 jit_solution(2211377206319435528)
XLA Ops:
  0.0 34.0 %pair_residual.1 = bf16[1,16,256]{2,1,0:T(8,128)(2,1)S(1)} custom-call(bf16[1,16,256]{2,1,0:T(8,128)(2,1)} %amp.1, bf16[1,16,2048]{2,1,0:T(8,128)(2,1)} %lad.1, bf16[1,16,2048]{2,1,0:T(8,128)(2,1)} %cyc.1, bf16[1,2,256]{2,1,0:T(2,128)(2,1)} %neu.1, f32[4,4]{1,0:T(4,128)} %rec_in.1, s32[4]{0:T(128)} %live_in.1), custom_call_target="tpu_custom_call" | custom-call | tf_op jit(solution)/shard_map/pair_residual/pallas_call | solution.py:468
  34.0 0.6 %copy.8 = bf16[1,16,256]{2,1,0:T(8,128)(2,1)} copy(bf16[1,16,256]{2,1,0:T(8,128)(2,1)S(1)} %pair_residual.1) | data formatting | bytes 16384

commit v5 on v4

--- a/solution.py
+++ b/solution.py
@@ -67,7 +67,7 @@
 
 
 SLOTS = 16
-PARTS = ((4, 9), (0, 4), (9, 12), (12, 16))
+PARTS = ((4, 9), (0, 4), (9, 13), (13, 16))
 LATE, EARLY = 8, 2
 HERE = 4
 
@@ -163,25 +163,30 @@
     def z_rows(slot):
         return pl.ds(pl.multiple_of(slot * 16, 16), 16)
 
+    def sender(k):
+        return max(k - 7, 0) if isinstance(k, int) else k - 7
+
     def z_copy(k, slot, to):
         lands = rem(slot - to + 32, 16)
         return send(
-            zbuf.at[z_rows(slot)], zbuf.at[z_rows(lands)], z_s.at[k], z_r.at[lands], at_z(to)
+            zbuf.at[z_rows(slot)], zbuf.at[z_rows(lands)], z_s.at[sender(k)],
+            z_r.at[div(lands + 3, 4)], at_z(to)
         )
 
     def n_copy(k, slot, to):
         lands = rem(slot - to + 32, 16)
         return send(
-            nz.at[pl.ds(slot, 1)], nz.at[pl.ds(lands, 1)], n_s.at[k], n_r.at[lands], at_z(to)
-        )
-
-    def z_wait(slot):
-        here = zbuf.at[z_rows(slot)]
-        send(here, here, z_s.at[0], z_r.at[slot], at_z(1)).wait_recv()
-
-    def n_wait(slot):
-        here = nz.at[pl.ds(slot, 1)]
-        send(here, here, n_s.at[0], n_r.at[slot], at_z(1)).wait_recv()
+            nz.at[pl.ds(slot, 1)], nz.at[pl.ds(lands, 1)], n_s.at[sender(k)],
+            n_r.at[div(lands + 3, 4)], at_z(to)
+        )
+
+    def z_wait(first, last):
+        here = zbuf.at[first * 16 : last * 16]
+        send(here, here, z_s.at[0], z_r.at[(first + 3) // 4], at_z(1)).wait_recv()
+
+    def n_wait(first, last):
+        here = nz.at[first:last]
+        send(here, here, n_s.at[0], n_r.at[(first + 3) // 4], at_z(1)).wait_recv()
 
     def goes_straight(source, to):
         return jnp.logical_and(
@@ -255,9 +260,7 @@
     get_neu.wait()
     get_rec.wait()
     each_straight(n_start)
-
-    @pl.loop(0, 8)
-    def _(k):
+    for k in range(8):
         n_copy(k, HERE, near_z(k)).start()
 
     def weights_out():
@@ -284,7 +287,7 @@
         src = zbuf.at[rows, pl.ds(pl.multiple_of(pyh * 128, 128), 128)]
         dst = abuf.at[rows, pl.ds(pl.multiple_of(e * 128, 128), 128)]
         dev = (pyh * 2 + yl, x * 32 + pyl * 16 + z)
-        return src, dst, a_s.at[part, k], a_r.at[part, e], dev
+        return src, dst, a_s, a_r.at[part], dev
 
     def is_self(k):
         return jnp.logical_and(co == yl, k == 3)
@@ -303,35 +306,28 @@
             def _():
                 send(src, dst, ss, rs, dev).start()
 
-    def a_sent(part):
-        @pl.loop(0, 4)
-        def _(k):
-            src, dst, ss, rs, dev = a_copy(part, k)
-
-            @pl.when(jnp.logical_not(is_self(k)))
-            def _():
-                send(src, dst, ss, rs, dev).wait_send()
+    def a_sent():
+        @pl.when(co == yl)
+        def _():
+            all_gone(abuf.at[:, 0:384], a_s)
+
+        @pl.when(co != yl)
+        def _():
+            all_gone(abuf, a_s)
 
     def a_wait(part):
-        rows = part_rows(part)
-
-        @pl.loop(0, 4)
-        def _(c):
-            dst = abuf.at[rows, pl.ds(pl.multiple_of(c * 128, 128), 128)]
-            send(dst, dst, a_s.at[0, 0], a_r.at[part, c], at_z(1)).wait_recv()
-
-    for slot in (5, 6, 7, 8):
-        z_wait(slot)
+        all_here(abuf.at[part_rows(part)], a_r.at[part])
+
+    z_wait(5, 9)
     each_high(z_start)
     a_start(0)
-    z_wait(0)
+    z_wait(0, 1)
     each_low(z_start)
-    for slot in (1, 2, 3):
-        z_wait(slot)
+    z_wait(1, 4)
     a_start(1)
-    n_wait(0)
+    n_wait(0, 1)
     each_low(n_start)
-    n_wait(8)
+    n_wait(5, 9)
     each_high(n_start)
 
     @pl.when(z >= LATE)
@@ -362,28 +358,20 @@
     all_gone(sall.at[0:48], s_s)
     all_gone(wts.at[0:480], w_s)
 
-    @pl.loop(0, 8)
-    def _(k):
-        z_copy(k, HERE, near_z(k)).wait_send()
-        n_copy(k, HERE, near_z(k)).wait_send()
+    all_gone(zbuf.at[0:128], z_s.at[0])
+    all_gone(nz.at[0:8], n_s.at[0])
 
     for part in (2, 3):
-        for slot in range(*PARTS[part]):
-            z_wait(slot)
+        z_wait(*PARTS[part])
         a_start(part)
 
     a_wait(0)
     a_wait(1)
     settle(0, 9)
 
-    @pl.loop(1, 4)
-    def _(k):
-        n_wait(k)
-        n_wait(k + 4)
-
-    @pl.loop(9, SLOTS)
-    def _(k):
-        n_wait(k)
+    n_wait(1, 4)
+    n_wait(9, 13)
+    n_wait(13, 16)
 
     place = lax.broadcasted_iota(jnp.int32, (32, 256), 0)
     stacked = jnp.zeros((32, 256), F32)
@@ -404,10 +392,10 @@
         each_high(sent)
 
     a_wait(2)
-    settle(9, 12)
+    settle(9, 13)
     a_wait(3)
 
-    settle(12, 16)
+    settle(13, 16)
     products = mm(wts[256:512, :], turned[...])
     for c in range(4):
         rows = slice(64 * c, 64 * c + 64)
@@ -444,8 +432,7 @@
         neutron = neutron + rec[e, c] * terms[16 * c : 16 * c + 16]
     neutron = swap_rows_lanes(neutron)
 
-    for part in range(4):
-        a_sent(part)
+    a_sent()
 
     all_gone(nall.at[0:224], n1_s)
     all_gone(fsend.at[0:240], f_s)
@@ -486,18 +473,18 @@
             pltpu.VMEM((256, 128), F32),
             pltpu.VMEM((16, 16, 128), F32),
             dma((4,)),
-            dma((15 + EARLY,)),
-            dma((16,)),
-            dma((15 + EARLY,)),
-            dma((16,)),
-            dma,
-            dma,
-            dma,
-            dma,
-            dma,
-            dma,
-            dma((4, 4)),
-            dma((4, 4)),
+            dma((8 + EARLY,)),
+            dma((5,)),
+            dma((8 + EARLY,)),
+            dma((5,)),
+            dma,
+            dma,
+            dma,
+            dma,
+            dma,
+            dma,
+            dma,
+            dma((4,)),
             dma,
             dma,
         ],

time: 34.8 us -> 34.2 us (0.983)
  Pallas kernels: 34 us -> 33.5 us
    pallas_call x1, Pallas kernels: 34 us -> 33.5 us  [local(): pl.pallas_call(kernel, out_shape=pltpu.VMEM((1, 16, 256), BF16), in_specs...]
where the time goes in v5:
time: 34.2 us; the launch traced here: 34.1 us
  Pallas kernels  33.5 us (98%)
  local copies, waits for them, and re-layouts  0.6 us (2%)
    pallas_call x1, Pallas kernels, local(): pl.pallas_call(kernel, out_shape=pltpu.VMEM((1, 16, 256), BF16), in_specs...  33.5 us

profile of v5, /device:TPU:1, one launch (start us, length us, event | category | flops | bytes accessed | tf_op | source)
XLA Modules:
  0.0 34.1 jit_solution(9916673483246208617)
XLA Ops:
  0.0 33.5 %pair_residual.1 = bf16[1,16,256]{2,1,0:T(8,128)(2,1)S(1)} custom-call(bf16[1,16,256]{2,1,0:T(8,128)(2,1)} %amp.1, bf16[1,16,2048]{2,1,0:T(8,128)(2,1)} %lad.1, bf16[1,16,2048]{2,1,0:T(8,128)(2,1)} %cyc.1, bf16[1,2,256]{2,1,0:T(2,128)(2,1)} %neu.1, f32[4,4]{1,0:T(4,128)} %rec_in.1, s32[4]{0:T(128)} %live_in.1), custom_call_target="tpu_custom_call" | custom-call | tf_op jit(solution)/shard_map/pair_residual/pallas_call | solution.py:455
  33.5 0.6 %copy.8 = bf16[1,16,256]{2,1,0:T(8,128)(2,1)} copy(bf16[1,16,256]{2,1,0:T(8,128)(2,1)S(1)} %pair_residual.1) | data formatting | bytes 16384

commit v6 on v5

--- a/solution.py
+++ b/solution.py
@@ -320,9 +320,9 @@
 
     z_wait(5, 9)
     each_high(z_start)
-    a_start(0)
     z_wait(0, 1)
     each_low(z_start)
+    a_start(0)
     z_wait(1, 4)
     a_start(1)
     n_wait(0, 1)

time: 34.2 us -> 34.2 us (level)
  no operation moved by 1% of the time
where the time goes in v6:
time: 34.2 us; the launch traced here: 34 us
  Pallas kernels  33.4 us (98%)
  local copies, waits for them, and re-layouts  0.6 us (2%)
    pallas_call x1, Pallas kernels, local(): pl.pallas_call(kernel, out_shape=pltpu.VMEM((1, 16, 256), BF16), in_specs...  33.4 us

profile of v6, /device:TPU:1, one launch (start us, length us, event | category | flops | bytes accessed | tf_op | source)
XLA Modules:
  0.0 34.0 jit_solution(2050559189224460104)
XLA Ops:
  0.0 33.4 %pair_residual.1 = bf16[1,16,256]{2,1,0:T(8,128)(2,1)S(1)} custom-call(bf16[1,16,256]{2,1,0:T(8,128)(2,1)} %amp.1, bf16[1,16,2048]{2,1,0:T(8,128)(2,1)} %lad.1, bf16[1,16,2048]{2,1,0:T(8,128)(2,1)} %cyc.1, bf16[1,2,256]{2,1,0:T(2,128)(2,1)} %neu.1, f32[4,4]{1,0:T(4,128)} %rec_in.1, s32[4]{0:T(128)} %live_in.1), custom_call_target="tpu_custom_call" | custom-call | tf_op jit(solution)/shard_map/pair_residual/pallas_call | solution.py:455
  33.4 0.6 %copy.8 = bf16[1,16,256]{2,1,0:T(8,128)(2,1)} copy(bf16[1,16,256]{2,1,0:T(8,128)(2,1)S(1)} %pair_residual.1) | data formatting | bytes 16384

commit v7 on v6

--- a/solution.py
+++ b/solution.py
@@ -93,8 +93,6 @@
     my_cols = pl.ds(pl.multiple_of(x * 512 + co * 256, 256), 256)
     own_l = pltpu.make_async_copy(lad.at[0, :, my_cols], wts.at[my_rows], w_r)
     own_c = pltpu.make_async_copy(cyc.at[0, :, my_cols], wts.at[low_rows], w_r)
-    get_amp.start()
-    get_live.start()
 
     def at_z(k):
         return (e, x * 32 + yl * 16 + lax.rem(z + k + 32, 16))
@@ -116,6 +114,8 @@
         pe, px = member(k)
         greet((pe, px * 32 + yl * 16 + z))
         greet(at_z(near_z((1, 5, 0, 2, 4, 6, 9, 13).index(k))))
+    get_amp.start()
+    get_live.start()
     for k in (3, 7, 8, 10, 11, 12, 14):
         pe, px = member(k)
         greet((pe, px * 32 + yl * 16 + z))

time: 34.2 us -> 34.4 us (level)
  no operation moved by 1% of the time
where the time goes in v7:
time: 34.4 us; the launch traced here: 34.3 us
  Pallas kernels  33.6 us (98%)
  local copies, waits for them, and re-layouts  0.6 us (2%)
    pallas_call x1, Pallas kernels, local(): pl.pallas_call(kernel, out_shape=pltpu.VMEM((1, 16, 256), BF16), in_specs...  33.6 us

profile of v7, /device:TPU:1, one launch (start us, length us, event | category | flops | bytes accessed | tf_op | source)
XLA Modules:
  0.0 34.3 jit_solution(4943327752809579795)
XLA Ops:
  0.0 33.6 %pair_residual.1 = bf16[1,16,256]{2,1,0:T(8,128)(2,1)S(1)} custom-call(bf16[1,16,256]{2,1,0:T(8,128)(2,1)} %amp.1, bf16[1,16,2048]{2,1,0:T(8,128)(2,1)} %lad.1, bf16[1,16,2048]{2,1,0:T(8,128)(2,1)} %cyc.1, bf16[1,2,256]{2,1,0:T(2,128)(2,1)} %neu.1, f32[4,4]{1,0:T(4,128)} %rec_in.1, s32[4]{0:T(128)} %live_in.1), custom_call_target="tpu_custom_call" | custom-call | tf_op jit(solution)/shard_map/pair_residual/pallas_call | solution.py:455
  33.7 0.6 %copy.8 = bf16[1,16,256]{2,1,0:T(8,128)(2,1)} copy(bf16[1,16,256]{2,1,0:T(8,128)(2,1)S(1)} %pair_residual.1) | data formatting | bytes 16384
